TPU v7x, 32 devices: a whole 2x2x4 slice. The times are simulated.
32 devices in a mesh: fsdp: 4 (over y, core), ctx: 4 (over z), tp: 2 (over x).
Axes of the slice: x: 2, y: 2, z: 4, core: 2. Of those that a mesh axis runs over, the one named last changes fastest.
Arguments:
- tokens: bfloat16 [8, 2048, 960], P('fsdp', ('ctx', 'tp')), may hold values from -6 to 6
- cotangent: bfloat16 [8, 2048, 960], P('fsdp', ('ctx', 'tp')), may hold values from -6 to 6
- input_gain: bfloat16 [960], P('fsdp'), may hold values from 0.099609375 to 1.8984375
- w_query: bfloat16 [960, 960], P('fsdp'), may hold values from -0.1875 to 0.1875
- w_keyval: bfloat16 [960, 640], P('fsdp'), may hold values from -0.1875 to 0.1875
- w_output: bfloat16 [960, 960], P('fsdp'), may hold values from -2 to 2
- middle_gain: bfloat16 [960], P('fsdp'), may hold values from 0.099609375 to 1.8984375
- w_gate: bfloat16 [960, 2560], P('fsdp', 'tp'), may hold values from -0.1875 to 0.1875
- w_up: bfloat16 [960, 2560], P('fsdp', 'tp'), may hold values from -0.1875 to 0.1875
- w_down: bfloat16 [960, 2560], P('fsdp', 'tp'), may hold values from -0.25 to 0.25
Outputs:
- result: bfloat16 [8, 2048, 960], P('fsdp', ('ctx', 'tp'))
- grad_tokens: float32 [8, 2048, 960], P('fsdp', ('ctx', 'tp'))
- grad_input_gain: float32 [960], P('fsdp')
- grad_w_query: float32 [960, 960], P('fsdp')
- grad_w_keyval: float32 [960, 640], P('fsdp')
- grad_w_output: float32 [960, 960], P('fsdp')
- grad_middle_gain: float32 [960], P('fsdp')
- grad_w_gate: float32 [960, 2560], P('fsdp', 'tp')
- grad_w_up: float32 [960, 2560], P('fsdp', 'tp')
- grad_w_down: float32 [960, 2560], P('fsdp', 'tp')
All inputs are finite; a program needn't handle non-finite values.
Results may differ from a plain program's by a relative error of at most 0.02.
Values may be sent and summed in bfloat16 or wider, within the bound.
A program may use at most 128 MiB of HBM per device.

v0:
```python
from functools import partial

import jax
import jax.numpy as jnp
from jax import lax
from jax.sharding import PartitionSpec as P

QUERY_HEADS = 15
KEYVAL_HEADS = 5
HEAD_WIDTH = 64
SEQUENCE_LENGTH = 2048
KEY_WIDTH = 320


EPS = 1e-05
THETA = 10000.0


def rope_tables(token_positions, first_place):
    half_width = HEAD_WIDTH // 2
    position = (first_place + lax.iota(jnp.int32, token_positions)).astype(jnp.float32)
    frequency = THETA ** (-(2.0 * lax.iota(jnp.int32, half_width).astype(jnp.float32)) / HEAD_WIDTH)
    angles = position[:, None] * frequency[None, :]
    return (jnp.cos(angles), jnp.sin(angles))


def apply_rotary(value_rows, cosine_table, sine_table, heads):
    half_width = HEAD_WIDTH // 2
    shaped = value_rows.reshape(value_rows.shape[:-1] + (heads, HEAD_WIDTH))
    leading = shaped[..., :half_width]
    trailing = shaped[..., half_width:]
    cosine_wide = cosine_table[:, None, :]
    sine_wide = sine_table[:, None, :]
    turned = jnp.concatenate(
        [
            leading * cosine_wide - trailing * sine_wide,
            trailing * cosine_wide + leading * sine_wide,
        ],
        -1,
    )
    return turned.reshape(value_rows.shape)


def normalize(value_rows):
    inverse_rms = lax.rsqrt(jnp.mean(value_rows * value_rows, -1, keepdims=True) + EPS)
    return (value_rows * inverse_rms, inverse_rms)


def norm_back(back_unit, unit_rows, inverse_rms):
    return inverse_rms * (
        back_unit - unit_rows * jnp.mean(back_unit * unit_rows, -1, keepdims=True)
    )


def to_heads(value_rows, sequence_count, token_positions):
    group_total = QUERY_HEADS // KEYVAL_HEADS
    return (
        value_rows.reshape(sequence_count, token_positions, KEYVAL_HEADS, group_total, HEAD_WIDTH)
        .transpose(0, 2, 3, 1, 4)
        .reshape(sequence_count * KEYVAL_HEADS, group_total * token_positions, HEAD_WIDTH)
    )


def from_heads(value_rows, sequence_count, token_positions):
    group_total = QUERY_HEADS // KEYVAL_HEADS
    return (
        value_rows.reshape(sequence_count, KEYVAL_HEADS, group_total, token_positions, HEAD_WIDTH)
        .transpose(0, 3, 1, 2, 4)
        .reshape(sequence_count, token_positions, QUERY_HEADS * HEAD_WIDTH)
    )


def per_sequence(value_rows, sequence_count):
    return value_rows.reshape((sequence_count, KEYVAL_HEADS) + value_rows.shape[1:])


def masked_scores(query_group, key_group, allowed):
    raw_scores = jnp.einsum("qd,kd->qk", query_group, key_group, preferred_element_type=jnp.float32)
    return jnp.where(allowed, raw_scores * HEAD_WIDTH ** (-0.5), -jnp.inf)


def head_forward(head_items, allowed):
    query_group, key_group, value_group = head_items
    scores = masked_scores(query_group, key_group, allowed)
    row_top = jnp.max(scores, -1, keepdims=True)
    lifted = jnp.exp(scores - row_top)
    row_total = jnp.sum(lifted, -1, keepdims=True)
    weights = (lifted / row_total).astype(jnp.bfloat16)
    mixed_heads = jnp.einsum("qk,kd->qd", weights, value_group, preferred_element_type=jnp.float32)
    return (mixed_heads, row_top[:, 0], row_total[:, 0])


def head_backward(head_items, allowed):
    query_group, key_group, value_group, back_mixed, row_top, row_total = head_items
    scores = masked_scores(query_group, key_group, allowed)
    weights = jnp.exp(scores - row_top[:, None]) / row_total[:, None]
    back_weights = jnp.einsum(
        "qd,kd->qk", back_mixed, value_group, preferred_element_type=jnp.float32
    )
    weighted_sum = jnp.sum(weights * back_weights, -1, keepdims=True)
    back_scores = (weights * (back_weights - weighted_sum)).astype(jnp.bfloat16)
    back_query = jnp.einsum(
        "qk,kd->qd", back_scores, key_group, preferred_element_type=jnp.float32
    ) * HEAD_WIDTH ** (-0.5)
    back_key = jnp.einsum(
        "qk,qd->kd", back_scores, query_group, preferred_element_type=jnp.float32
    ) * HEAD_WIDTH ** (-0.5)
    back_value = jnp.einsum(
        "qk,qd->kd", weights.astype(jnp.bfloat16), back_mixed, preferred_element_type=jnp.float32
    )
    return (back_query, back_key, back_value)


def on_device(
    tokens, cotangent, input_gain, w_query, w_keyval, w_output, middle_gain, w_gate, w_up, w_down
):
    sequence_count = tokens.shape[0]
    token_positions = tokens.shape[1]
    group_total = QUERY_HEADS // KEYVAL_HEADS
    place_index = lax.axis_index("ctx") * lax.axis_size("tp") + lax.axis_index("tp")
    first_place = place_index * token_positions
    cosine_table, sine_table = rope_tables(token_positions, first_place)
    query_place = first_place + lax.iota(jnp.int32, group_total * token_positions) % token_positions
    allowed = lax.iota(jnp.int32, SEQUENCE_LENGTH)[None, :] <= query_place[:, None]
    full_gain_one, full_query, full_keyval, full_output = (
        lax.all_gather(input_gain, "fsdp", axis=0, tiled=True),
        lax.all_gather(w_query, "fsdp", axis=0, tiled=True),
        lax.all_gather(w_keyval, "fsdp", axis=0, tiled=True),
        lax.all_gather(w_output, "fsdp", axis=0, tiled=True),
    )
    gain_one = full_gain_one.astype(jnp.float32)
    inputs = tokens.astype(jnp.float32)
    unit_one, inverse_one = normalize(inputs)
    normed_one = (unit_one * gain_one).astype(jnp.bfloat16)
    query_raw = jnp.dot(normed_one, full_query, preferred_element_type=jnp.float32)
    keyval_unrotated = jnp.dot(normed_one, full_keyval, preferred_element_type=jnp.float32)
    query_low = apply_rotary(query_raw, cosine_table, sine_table, QUERY_HEADS).astype(jnp.bfloat16)
    keyval_low = jnp.concatenate(
        [
            apply_rotary(keyval_unrotated[..., :KEY_WIDTH], cosine_table, sine_table, KEYVAL_HEADS),
            keyval_unrotated[..., KEY_WIDTH:],
        ],
        -1,
    ).astype(jnp.bfloat16)
    keyval_gathered = lax.all_gather(keyval_low, ("ctx", "tp"), axis=1, tiled=True)
    query_heads = to_heads(query_low, sequence_count, token_positions)
    stacked = (
        keyval_gathered.reshape(sequence_count, SEQUENCE_LENGTH, 2, KEYVAL_HEADS, HEAD_WIDTH)
        .transpose(2, 0, 3, 1, 4)
        .reshape(2, sequence_count * KEYVAL_HEADS, SEQUENCE_LENGTH, HEAD_WIDTH)
    )
    key_heads = stacked[0]
    value_heads = stacked[1]
    mixed_heads, row_top, row_total = lax.map(
        partial(head_forward, allowed=allowed), (query_heads, key_heads, value_heads)
    )
    mixed_low = from_heads(mixed_heads, sequence_count, token_positions).astype(jnp.bfloat16)
    attention_out = jnp.dot(mixed_low, full_output, preferred_element_type=jnp.float32)
    middle = inputs + attention_out
    full_gate, full_up, full_down, full_gain_two = (
        lax.all_gather(w_gate, "fsdp", axis=0, tiled=True),
        lax.all_gather(w_up, "fsdp", axis=0, tiled=True),
        lax.all_gather(w_down, "fsdp", axis=0, tiled=True),
        lax.all_gather(middle_gain, "fsdp", axis=0, tiled=True),
    )
    gain_two = full_gain_two.astype(jnp.float32)
    unit_two, inverse_two = normalize(middle)
    normed_two = (unit_two * gain_two).astype(jnp.bfloat16)
    pair_rows, pair_cotangent = (
        lax.all_gather(normed_two, "tp", axis=1, tiled=True),
        lax.all_gather(cotangent, "tp", axis=1, tiled=True),
    )
    gate_proj = jnp.dot(pair_rows, full_gate, preferred_element_type=jnp.float32)
    up_proj = jnp.dot(pair_rows, full_up, preferred_element_type=jnp.float32)
    sigmoid_gate = jax.nn.sigmoid(gate_proj)
    swish_gate = gate_proj * sigmoid_gate
    hidden = (swish_gate * up_proj).astype(jnp.bfloat16)
    branch_part = jnp.einsum("spf,df->spd", hidden, full_down, preferred_element_type=jnp.float32)
    feed_out = lax.psum_scatter(
        branch_part.astype(jnp.bfloat16), "tp", scatter_dimension=1, tiled=True
    ).astype(jnp.float32)
    result = (middle + feed_out).astype(jnp.bfloat16)
    back_hidden = jnp.dot(pair_cotangent, full_down, preferred_element_type=jnp.float32)
    back_gate = (
        back_hidden * up_proj * sigmoid_gate * (1.0 + gate_proj * (1.0 - sigmoid_gate))
    ).astype(jnp.bfloat16)
    back_up = (back_hidden * swish_gate).astype(jnp.bfloat16)
    grad_down = jnp.einsum(
        "spd,spf->df", pair_cotangent, hidden, preferred_element_type=jnp.float32
    )
    grad_gate = jnp.einsum("spd,spf->df", pair_rows, back_gate, preferred_element_type=jnp.float32)
    grad_up = jnp.einsum("spd,spf->df", pair_rows, back_up, preferred_element_type=jnp.float32)
    back_normed_part = jnp.einsum(
        "spf,df->spd", back_gate, full_gate, preferred_element_type=jnp.float32
    ) + jnp.einsum("spf,df->spd", back_up, full_up, preferred_element_type=jnp.float32)
    back_normed_two = lax.psum_scatter(back_normed_part, "tp", scatter_dimension=1, tiled=True)
    grad_gain_two = jnp.sum(back_normed_two * unit_two, axis=(0, 1))
    back_middle = cotangent.astype(jnp.float32) + norm_back(
        back_normed_two * gain_two, unit_two, inverse_two
    )
    back_attention = back_middle.astype(jnp.bfloat16)
    grad_output = jnp.einsum(
        "spq,spd->qd", mixed_low, back_attention, preferred_element_type=jnp.float32
    )
    back_mixed = jnp.einsum(
        "spd,qd->spq", back_attention, full_output, preferred_element_type=jnp.float32
    ).astype(jnp.bfloat16)

    def attend_back(carried, sequence_items):
        back_query, back_key, back_value = lax.map(
            partial(head_backward, allowed=allowed), sequence_items
        )
        back_keyval = (
            jnp.stack([back_key, back_value])
            .transpose(2, 0, 1, 3)
            .reshape(SEQUENCE_LENGTH, 2 * KEY_WIDTH)
        )
        owned_rows = lax.psum_scatter(
            back_keyval.astype(jnp.bfloat16), ("ctx", "tp"), scatter_dimension=0, tiled=True
        ).astype(jnp.float32)
        return (carried, (back_query, owned_rows))

    sequence_items = tuple(
        (
            per_sequence(value_rows, sequence_count)
            for value_rows in (
                query_heads,
                key_heads,
                value_heads,
                to_heads(back_mixed, sequence_count, token_positions),
                row_top,
                row_total,
            )
        )
    )
    unused, (query_gradient_full, owned_tokens_full) = lax.scan(
        attend_back, jnp.zeros((), jnp.float32), sequence_items
    )
    back_query_rows = from_heads(
        query_gradient_full.reshape(
            (sequence_count * KEYVAL_HEADS,) + query_gradient_full.shape[2:]
        ),
        sequence_count,
        token_positions,
    )
    back_query_low = apply_rotary(back_query_rows, cosine_table, -sine_table, QUERY_HEADS).astype(
        jnp.bfloat16
    )
    back_keyval_low = jnp.concatenate(
        [
            apply_rotary(
                owned_tokens_full[..., :KEY_WIDTH], cosine_table, -sine_table, KEYVAL_HEADS
            ),
            owned_tokens_full[..., KEY_WIDTH:],
        ],
        -1,
    ).astype(jnp.bfloat16)
    grad_query = jnp.einsum(
        "spd,spq->dq", normed_one, back_query_low, preferred_element_type=jnp.float32
    )
    grad_keyval = jnp.einsum(
        "spd,spk->dk", normed_one, back_keyval_low, preferred_element_type=jnp.float32
    )
    back_normed_one = jnp.einsum(
        "spq,dq->spd", back_query_low, full_query, preferred_element_type=jnp.float32
    ) + jnp.einsum("spk,dk->spd", back_keyval_low, full_keyval, preferred_element_type=jnp.float32)
    grad_gain_one = jnp.sum(back_normed_one * unit_one, axis=(0, 1))
    back_inputs = back_middle + norm_back(back_normed_one * gain_one, unit_one, inverse_one)
    attention_term = jnp.concatenate([grad_query, grad_keyval, grad_output], 1)
    feed_term = jnp.concatenate([grad_gate, grad_up, grad_down], 1)
    attention_total, gain_one_total, gain_two_total = (
        lax.psum(attention_term.astype(jnp.bfloat16), ("ctx", "tp")).astype(jnp.float32),
        lax.psum(grad_gain_one.astype(jnp.bfloat16), ("ctx", "tp")).astype(jnp.float32),
        lax.psum(grad_gain_two.astype(jnp.bfloat16), ("ctx", "tp")).astype(jnp.float32),
    )
    feed_total = lax.psum(feed_term.astype(jnp.bfloat16), "ctx")
    attention_share, feed_share, gain_one_share, gain_two_share = (
        lax.psum_scatter(
            attention_total.astype(jnp.bfloat16), "fsdp", scatter_dimension=0, tiled=True
        ).astype(jnp.float32),
        lax.psum_scatter(feed_total, "fsdp", scatter_dimension=0, tiled=True).astype(jnp.float32),
        lax.psum_scatter(
            gain_one_total.astype(jnp.bfloat16), "fsdp", scatter_dimension=0, tiled=True
        ).astype(jnp.float32),
        lax.psum_scatter(
            gain_two_total.astype(jnp.bfloat16), "fsdp", scatter_dimension=0, tiled=True
        ).astype(jnp.float32),
    )
    query_width = full_query.shape[1]
    keyval_width = full_keyval.shape[1]
    hidden_width = full_gate.shape[1]
    share_query = attention_share[:, :query_width]
    share_keyval = attention_share[:, query_width : query_width + keyval_width]
    share_output = attention_share[:, query_width + keyval_width :]
    share_gate = feed_share[:, :hidden_width]
    share_up = feed_share[:, hidden_width : 2 * hidden_width]
    share_down = feed_share[:, 2 * hidden_width :]
    return (
        result,
        back_inputs,
        gain_one_share,
        share_query,
        share_keyval,
        share_output,
        gain_two_share,
        share_gate,
        share_up,
        share_down,
    )


def solution(mesh):
    in_specs = (
        P("fsdp", ("ctx", "tp"), None),
        P("fsdp", ("ctx", "tp"), None),
        P("fsdp"),
        P("fsdp", None),
        P("fsdp", None),
        P("fsdp", None),
        P("fsdp"),
        P("fsdp", "tp"),
        P("fsdp", "tp"),
        P("fsdp", "tp"),
    )
    out_specs = (
        P("fsdp", ("ctx", "tp"), None),
        P("fsdp", ("ctx", "tp"), None),
        P("fsdp"),
        P("fsdp", None),
        P("fsdp", None),
        P("fsdp", None),
        P("fsdp"),
        P("fsdp", "tp"),
        P("fsdp", "tp"),
        P("fsdp", "tp"),
    )
    return jax.shard_map(
        on_device, mesh=mesh, in_specs=in_specs, out_specs=out_specs, check_vma=False
    )
```

profile of v0, /device:TPU:0, one launch (start us, length us, event | category | flops | bytes accessed | tf_op | source)
XLA Modules:
  0.0 1055.7 jit_solution(356635097389830232)
XLA Ops:
  12.4 8.3 all-reduce.6
  37.3 16.2 %all-gather.10.cloned.1.call-done = bf16[960,960]{1,0:T(8,128)(2,1)} async-done(((bf16[240,960]{1,0:T(8,128)(2,1)}), bf16[960,960]{1,0:T(8,128)(2,1)}) %all-gather.10.cloned.1.call-update) | async-done | bytes 1843216 | tf_op jit(solution)/shard_map/all_gather | solution.py:127
  58.6 84.0 %all-gather.14.cloned.1.call-done = bf16[2,2048,640]{2,1,0:T(8,128)(2,1)} async-done(((bf16[2,256,640]{2,1,0:T(8,128)(2,1)}), bf16[2,2048,640]{2,1,0:T(8,128)(2,1)}) %all-gather.14.cloned.1.call-update) | async-done | bytes 5242896 | tf_op jit(solution)/shard_map/all_gather | solution.py:145
  142.6 8.0 copy.72
  150.6 7.3 slice_bitcast_fusion
  157.9 80.6 %while.43 = (s32[]{:T(128)}, bf16[10,768,64]{1,2,0:T(8,128)(2,1)S(1)}, f32[10,768]{1,0:T(8,128)S(1)}, f32[10,768]{1,0:T(8,128)S(1)}, bf16[10,768,64]{2,1,0:T(8,1...) while((s32[]{:T(128)}, ...), condition=%wide.region_4.5_spmd.clone, body=%wide.region_1.4_spmd.clone.sunk | while | flops 426244608 | bytes 19846260 | solution.py:154
  249.1 7.6 fusion.58
  256.6 26.5 %all-gather.18.cloned.1.call-done = bf16[2,512,960]{1,2,0:T(8,128)(2,1)} async-done(((bf16[2,256,960]{1,2,0:T(8,128)(2,1)}), bf16[2,512,960]{1,2,0:T(8,128)(2,1)}) %all-gather.18.cloned.1.call-update) | async-done | bytes 1966096 | tf_op jit(solution)/shard_map/all_gather | solution.py:170
  283.1 7.6 fusion.64
  290.7 18.6 %all-gather.20.cloned.1.call-done = bf16[960,1280]{1,0:T(8,128)(2,1)} async-done(((bf16[240,1280]{1,0:T(8,128)(2,1)}), bf16[960,1280]{1,0:T(8,128)(2,1)}) %all-gather.20.cloned.1.call-update) | async-done | bytes 2457616 | tf_op jit(solution)/shard_map/all_gather | solution.py:161
  309.4 11.9 %multiply_convert_fusion.2 = (bf16[2,512,1280]{2,1,0:T(8,128)(2,1)S(1)}, bf16[2,512,1280]{2,1,0:T(8,128)(2,1)S(1)}, bf16[2,512,1280]{2,1,0:T(8,128)(2,1)}) fusion(f32[2,512,1280]{2,1,0:T(8,128)} %fusion.58, f32[2,512,1280]{2,1,0:T(8,128)} %fusion.64, bf16[2,512,960]{1,2,0:T(8,128)(2,1)} %all-gather.18.cloned.1.call-done, ...), kind=kOutput, calls=%fused_computation.71 | convolution fusion | flops 2536243200 | bytes 22773760 | tf_op jit(solution)/shard_map/dot_general | solution.py:173
  352.2 29.6 %reduce-scatter.8.cloned.1.call-done = f32[2,256,960]{1,2,0:T(8,128)} async-done(((f32[2,512,960]{1,2,0:T(8,128)}), f32[2,256,960]{1,2,0:T(8,128)}) %reduce-scatter.8.cloned.1.call-update) | async-done | bytes 1966096 | tf_op jit(solution)/shard_map/reduce_scatter | solution.py:196
  384.5 30.1 %reduce-scatter.6.cloned.1.call-done = bf16[2,256,960]{1,2,0:T(8,128)(2,1)} async-done(((bf16[2,512,960]{1,2,0:T(8,128)(2,1)}), bf16[2,256,960]{1,2,0:T(8,128)(2,1)}) %reduce-scatter.6.cloned.1.call-update) | async-done | bytes 983056 | tf_op jit(solution)/shard_map/reduce_scatter | solution.py:179
  421.2 340.2 %while.45 = (s32[]{:T(128)}, f32[2,5,768,64]{2,3,1,0:T(8,128)}, f32[2,256,640]{1,2,0:T(8,128)}, bf16[2,5,768,64]{3,2,1,0:T(8,128)(2,1)}, bf16[2,5,2048,64]{2,3,1...) while((s32[]{:T(128)}, f32[2,5,768,64]{2,3,1,0:T(8,128)}, ...), condition=%wide.region_14.15_spmd.clone, body=%wide.region_9.14_spmd.clone.sunk | while | flops 1025588480 | bytes 125203080 | solution.py:236
  435.4 79.8 %while.46 = (s32[]{:T(128)}, f32[5,768,64]{1,2,0:T(8,128)}, bf16[5,2048,64]{1,2,0:T(8,128)(2,1)}, bf16[5,2048,64]{1,2,0:T(8,128)(2,1)}, bf16[5,768,64]{2,1,0:T(8...) while((s32[]{:T(128)}, f32[5,768,64]{1,2,0:T(8,128)}, ...), condition=%wide.region_12.12_spmd, body=%wide.region_10.11_spmd.sunk | while | flops 1022541056 | bytes 79656208 | solution.py:210
  521.0 68.8 %reduce-scatter.14.cloned.1.call-done = bf16[256,640]{0,1:T(8,128)(2,1)} async-done(((bf16[2048,640]{0,1:T(8,128)(2,1)}), bf16[256,640]{0,1:T(8,128)(2,1)}) %reduce-scatter.14.cloned.1.call-update) | async-done | bytes 327696 | tf_op jit(solution)/shard_map/while/body/eval_jaxpr/reduce_scatter | solution.py:218
  605.8 79.8 %while.46 = (s32[]{:T(128)}, f32[5,768,64]{1,2,0:T(8,128)}, bf16[5,2048,64]{1,2,0:T(8,128)(2,1)}, bf16[5,2048,64]{1,2,0:T(8,128)(2,1)}, bf16[5,768,64]{2,1,0:T(8...) while((s32[]{:T(128)}, f32[5,768,64]{1,2,0:T(8,128)}, ...), condition=%wide.region_12.12_spmd, body=%wide.region_10.11_spmd.sunk | while | flops 1022541056 | bytes 79656208 | solution.py:210
  691.5 67.8 %reduce-scatter.14.cloned.1.call-done = bf16[256,640]{0,1:T(8,128)(2,1)} async-done(((bf16[2048,640]{0,1:T(8,128)(2,1)}), bf16[256,640]{0,1:T(8,128)(2,1)}) %reduce-scatter.14.cloned.1.call-update) | async-done | bytes 327696 | tf_op jit(solution)/shard_map/while/body/eval_jaxpr/reduce_scatter | solution.py:218
  779.8 9.3 concatenate.38
  789.2 39.9 %reduce-scatter.12.cloned.1.call-done = bf16[240,3840]{1,0:T(8,128)(2,1)} async-done(((bf16[960,3840]{1,0:T(8,128)(2,1)}), bf16[240,3840]{1,0:T(8,128)(2,1)}) %reduce-scatter.12.cloned.1.call-update) | async-done | bytes 1843216 | tf_op jit(solution)/shard_map/reduce_scatter | solution.py:281
  841.5 21.5 %all-reduce.4 = (bf16[240]{0:T(256)(128)(2,1)S(1)}, bf16[240]{0:T(256)(128)(2,1)S(1)}) all-reduce(bf16[240]{0:T(256)(128)(2,1)S(1)} %dynamic-slice.3, bf16[240]{0:T(256)(128)(2,1)S(1)} %dynamic-slice.5), channel_id=1, replica_groups=mesh['fsdp'=4,'ctx'=4,'tp'=2] {'ctx','tp'}, use_global_device_ids=true, to_apply=%region_17.18 | all-reduce | flops 480 | bytes 1920 | tf_op jit(solution)/shard_map/psum | solution.py:273
  864.1 16.9 %reduce-scatter.10.cloned.1.call-done = bf16[240,2560]{1,0:T(8,128)(2,1)} async-done(((bf16[960,2560]{1,0:T(8,128)(2,1)}), bf16[240,2560]{1,0:T(8,128)(2,1)}) %reduce-scatter.10.cloned.1.call-update) | async-done | bytes 1228816 | tf_op jit(solution)/shard_map/reduce_scatter | solution.py:278
  884.3 77.3 %all-reduce.12.cloned.1.call-done = bf16[240,3840]{1,0:T(8,128)(2,1)} async-done(((bf16[240,3840]{1,0:T(8,128)(2,1)}), bf16[240,3840]{1,0:T(8,128)(2,1)}) %all-reduce.12.cloned.1.call-update) | async-done | bytes 1843216 | tf_op jit(solution)/shard_map/psum | solution.py:276
  965.0 80.2 %all-reduce.10.cloned.1.call-done = bf16[240,2560]{1,0:T(8,128)(2,1)} async-done(((bf16[240,2560]{1,0:T(8,128)(2,1)}), bf16[240,2560]{1,0:T(8,128)(2,1)}) %all-reduce.10.cloned.1.call-update) | async-done | bytes 1228816 | tf_op jit(solution)/shard_map/psum | solution.py:272
  (457 shorter events, 400.7 us)
Async XLA Ops:
  7.2 22.9 %copy-start.11 = (bf16[2,256,960]{1,2,0:T(8,128)(2,1)S(1)}, bf16[2,256,960]{1,2,0:T(8,128)(2,1)}, u32[]{:S(2)}) copy-start(bf16[2,256,960]{1,2,0:T(8,128)(2,1)} %param.16) | copy-start | bytes 2949124
  7.2 22.9 %all-gather.12.cloned.1.call-start = ((), (), s32[]{:S(2)}) async-start(), calls=%async_computation.6 | async-start | bytes 1536000 | tf_op jit(solution)/shard_map/all_gather | solution.py:128
  7.9 45.6 %all-gather.10.cloned.1.call-start = ((), (), s32[]{:S(2)}) async-start(), calls=%async_computation.5 | async-start | bytes 2457600 | tf_op jit(solution)/shard_map/all_gather | solution.py:127
  8.7 133.9 %all-gather.14.cloned.1.call-start = ((), (), s32[]{:S(2)}) async-start(), calls=%async_computation.7 | async-start | bytes 5898240 | tf_op jit(solution)/shard_map/all_gather | solution.py:145
  20.8 32.8 %copy-start.28 = (f32[960]{0:T(1024)}, f32[960]{0:T(1024)S(1)}, u32[]{:S(2)}) copy-start(f32[960]{0:T(1024)S(1)} %convert_element_type.123) | copy-start | bytes 11524
  22.2 31.3 %copy-start.31 = (f32[2,256]{1,0:T(2,128)}, f32[2,256]{1,0:T(2,128)S(1)}, u32[]{:S(2)}) copy-start(f32[2,256]{1,0:T(2,128)S(1)} %add_rsqrt_fusion.1) | copy-start | bytes 6148
  23.0 33.4 %copy-start.21 = (f32[256,32]{0,1:T(8,128)}, f32[256,32]{0,1:T(8,128)S(1)}, u32[]{:S(2)}) copy-start(f32[256,32]{0,1:T(8,128)S(1)} %get-tuple-element.374) | copy-start | bytes 98308
  34.4 208.9 %all-gather.16.cloned.1.call-start = ((), (), s32[]{:S(2)}) async-start(), calls=%async_computation.8 | async-start | bytes 2457600 | tf_op jit(solution)/shard_map/all_gather | solution.py:129
  35.0 214.1 %all-gather.26.cloned.1.call-start = ((), (), s32[]{:S(2)}) async-start(), calls=%async_computation.14 | async-start | bytes 2949120 | tf_op jit(solution)/shard_map/all_gather | solution.py:171
  35.6 213.5 %all-gather.24.cloned.1.call-start = ((), (), s32[]{:S(2)}) async-start(), calls=%async_computation.12 | async-start | bytes 3072000 | tf_op jit(solution)/shard_map/all_gather | solution.py:163
  36.2 220.5 %all-gather.22.cloned.1.call-start = ((), (), s32[]{:S(2)}) async-start(), calls=%async_computation.11 | async-start | bytes 3072000 | tf_op jit(solution)/shard_map/all_gather | solution.py:162
  36.9 246.2 %all-gather.18.cloned.1.call-start = ((), (), s32[]{:S(2)}) async-start(), calls=%async_computation.9 | async-start | bytes 2949120 | tf_op jit(solution)/shard_map/all_gather | solution.py:170
  247.7 61.7 %all-gather.20.cloned.1.call-start = ((), (), s32[]{:S(2)}) async-start(), calls=%async_computation.10 | async-start | bytes 3072000 | tf_op jit(solution)/shard_map/all_gather | solution.py:161
  248.5 133.4 %reduce-scatter.8.cloned.1.call-start = ((), (), s32[]{:S(2)}) async-start(), calls=%async_computation.15 | async-start | bytes 5898240 | tf_op jit(solution)/shard_map/reduce_scatter | solution.py:196
  329.7 84.9 %reduce-scatter.6.cloned.1.call-start = ((), (), s32[]{:S(2)}) async-start(), calls=%async_computation.13 | async-start | bytes 2949120 | tf_op jit(solution)/shard_map/reduce_scatter | solution.py:179
  352.2 62.3 %copy-start.10 = (bf16[2,256,960]{1,2,0:T(8,128)(2,1)S(1)}, bf16[2,256,960]{1,2,0:T(8,128)(2,1)}, u32[]{:S(2)}) copy-start(bf16[2,256,960]{1,2,0:T(8,128)(2,1)} %param.17) | copy-start | bytes 2949124
  421.4 168.5 %reduce-scatter.14.cloned.1.call-start = ((), (), s32[]{:S(2)}) async-start(), calls=%async_computation.20 | async-start | bytes 2949120 | tf_op jit(solution)/shard_map/while/body/eval_jaxpr/reduce_scatter | solution.py:218
  518.7 71.1 %copy-start.13 = (f32[2,256,640]{1,2,0:T(8,128)S(1)}, f32[2,256,640]{1,2,0:T(8,128)}, u32[]{:S(2)}) copy-start(f32[2,256,640]{1,2,0:T(8,128)} %get-tuple-element.691) | copy-start | bytes 3932164 | tf_op jit(solution)/shard_map/while
  591.9 167.4 %reduce-scatter.14.cloned.1.call-start = ((), (), s32[]{:S(2)}) async-start(), calls=%async_computation.20 | async-start | bytes 2949120 | tf_op jit(solution)/shard_map/while/body/eval_jaxpr/reduce_scatter | solution.py:218
  689.2 70.1 %copy-start.13 = (f32[2,256,640]{1,2,0:T(8,128)S(1)}, f32[2,256,640]{1,2,0:T(8,128)}, u32[]{:S(2)}) copy-start(f32[2,256,640]{1,2,0:T(8,128)} %get-tuple-element.691) | copy-start | bytes 3932164 | tf_op jit(solution)/shard_map/while
  761.4 67.7 %reduce-scatter.12.cloned.1.call-start = ((), (), s32[]{:S(2)}) async-start(), calls=%async_computation.18 | async-start | bytes 9216000 | tf_op jit(solution)/shard_map/reduce_scatter | solution.py:281
  762.0 119.0 %reduce-scatter.10.cloned.1.call-start = ((), (), s32[]{:S(2)}) async-start(), calls=%async_computation.16 | async-start | bytes 6144000 | tf_op jit(solution)/shard_map/reduce_scatter | solution.py:278
  789.2 172.5 %all-reduce.12.cloned.1.call-start = ((), (), s32[]{:S(2)}) async-start(), calls=%async_computation.19 | async-start | bytes 3686400 | tf_op jit(solution)/shard_map/psum | solution.py:276
  829.2 216.1 %all-reduce.10.cloned.1.call-start = ((), (), s32[]{:S(2)}) async-start(), calls=%async_computation.17 | async-start | bytes 2457600 | tf_op jit(solution)/shard_map/psum | solution.py:272
  (83 other events, 196.8 us)
Sparse Core Ops, SparseCore 0:
  9.6 20.4 all-gather.11
  31.6 21.8 all-gather.9
  56.3 86.2 all-gather.13
  144.0 20.0 all-gather.15
  165.4 31.5 all-gather.25
  198.5 24.6 all-gather.23
  224.8 24.5 all-gather.21
  251.5 31.5 all-gather.17
  284.7 24.6 all-gather.19
  329.8 51.9 reduce-scatter.7
  384.1 30.3 reduce-scatter.5
  518.9 70.8 reduce-scatter.13
  689.3 69.9 reduce-scatter.13
  764.5 64.6 reduce-scatter.11
  831.7 49.2 reduce-scatter.9
  883.2 78.3 all-reduce.11
  965.1 80.1 all-reduce.9
where the time goes:
time: 1060 us
  waiting for transfers between devices  568 us (54%)
  matrix products  260 us (25%)
  local copies, waits for them, and re-layouts  112 us (11%)
  other arithmetic  60.4 us (6%)
  blocking collectives  35.6 us (3%)
  between operations  16.1 us (2%)
    reduce_scatter x2, waiting for transfers between devices, attend_back(): lax.psum_scatter(back_keyval.astype(jnp.bfloat16), ('ctx', 'tp'), scatter...  137 us
    all_gather x1, waiting for transfers between devices, on_device(): lax.all_gather(keyval_low, ('ctx', 'tp'), axis=1, tiled=True)  84 us
    psum x1, waiting for transfers between devices, on_device(): lax.psum(attention_term.astype(jnp.bfloat16), ('ctx', 'tp'))  80.2 us
    psum x1, waiting for transfers between devices, on_device(): feed_total = lax.psum(feed_term.astype(jnp.bfloat16), 'ctx')  77.3 us
    dot_general x20, matrix products, masked_scores(): jnp.einsum('qd,kd->qk', query_group, key_group, preferred_element_type=jn...  60.3 us
    reduce_scatter x1, waiting for transfers between devices, on_device(): lax.psum_scatter(feed_total, 'fsdp', scatter_dimension=0, tiled=True)  39.9 us
    dot_general x10, matrix products, head_forward(): jnp.einsum('qk,kd->qd', weights, value_group, preferred_element_type=jnp....  33.4 us
    reduce_scatter x1, waiting for transfers between devices, on_device(): lax.psum_scatter(branch_part.astype(jnp.bfloat16), 'tp', scatter_dimensio...  30.1 us
  transfers between devices with their start and end apart: 17, of which 13 were waited for; matrix products, arithmetic and copies ran while one was open for 19% of the time, Pallas kernels for 0%

commit v1 on v0

v1 whole, which is shorter than its diff:
```python
import jax
import jax.numpy as jnp
from jax import lax
from jax.experimental import pallas as pl
from jax.experimental.pallas import tpu as pltpu
from jax.sharding import PartitionSpec as P

QUERY_HEADS = 15
KEYVAL_HEADS = 5
GROUP = QUERY_HEADS // KEYVAL_HEADS
HEAD_WIDTH = 64
HALF = HEAD_WIDTH // 2
KEY_WIDTH = 320
QUERY_WIDTH = QUERY_HEADS * HEAD_WIDTH
SCALE = HEAD_WIDTH ** (-0.5)

EPS = 1e-05
THETA = 10000.0
VMEM_LIMIT = 40 * 1024 * 1024


def dot(left, right, left_dim, right_dim):
    return lax.dot_general(
        left, right, (((left_dim,), (right_dim,)), ((), ())), preferred_element_type=jnp.float32
    )


def rope_tables(token_positions, first_place):
    position = (first_place + lax.iota(jnp.int32, token_positions)).astype(jnp.float32)
    frequency = THETA ** (-(2.0 * lax.iota(jnp.int32, HALF).astype(jnp.float32)) / HEAD_WIDTH)
    angles = frequency[:, None] * position[None, :]
    return (jnp.cos(angles), jnp.sin(angles))


def apply_rotary(rows, cosine, sine):
    shaped = rows.reshape(-1, 2, HALF, rows.shape[-1])
    leading = shaped[:, 0]
    trailing = shaped[:, 1]
    return jnp.stack(
        [leading * cosine - trailing * sine, trailing * cosine + leading * sine], 1
    ).reshape(rows.shape)


def normalize(value_rows):
    inverse_rms = lax.rsqrt(jnp.mean(value_rows * value_rows, -1, keepdims=True) + EPS)
    return (value_rows * inverse_rms, inverse_rms)


def norm_back(back_unit, unit_rows, inverse_rms):
    return inverse_rms * (
        back_unit - unit_rows * jnp.mean(back_unit * unit_rows, -1, keepdims=True)
    )


def causal(scores):
    key_place = lax.broadcasted_iota(jnp.int32, scores.shape, 0)
    query_place = lax.broadcasted_iota(jnp.int32, scores.shape, 1)
    return jnp.where(key_place <= query_place, scores, -jnp.inf)


def forward_kernel(query_ref, key_ref, value_ref, mixed_ref, lse_ref):
    place = lax.axis_index("ctx")
    queries = [query_ref[g] * jnp.bfloat16(SCALE) for g in range(GROUP)]

    def scores_of(keys_turned, g, masked):
        scores = dot(keys_turned, queries[g], 1, 0)
        return causal(scores) if masked else scores

    def first():
        keys_turned = key_ref[place, 0, 0].T
        values = value_ref[place, 0, 0]
        carried = []
        for g in range(GROUP):
            scores = scores_of(keys_turned, g, True)
            top = jnp.max(scores, 0, keepdims=True)
            lifted = jnp.exp(scores - top)
            total = jnp.sum(lifted, 0, keepdims=True)
            carried += [top, total, dot(values, lifted.astype(jnp.bfloat16), 1, 0)]
        return tuple(carried)

    def step(block, carried):
        keys_turned = key_ref[block, 0, 0].T
        values = value_ref[block, 0, 0]
        later = []
        for g in range(GROUP):
            top, total, mixed = carried[3 * g : 3 * g + 3]
            scores = scores_of(keys_turned, g, False)
            new_top = jnp.maximum(top, jnp.max(scores, 0, keepdims=True))
            lifted = jnp.exp(scores - new_top)
            shrink = jnp.exp(top - new_top)
            later += [
                new_top,
                total * shrink + jnp.sum(lifted, 0, keepdims=True),
                mixed * shrink + dot(values, lifted.astype(jnp.bfloat16), 1, 0),
            ]
        return tuple(later)

    carried = lax.fori_loop(0, place, step, first())
    for g in range(GROUP):
        top, total, mixed = carried[3 * g : 3 * g + 3]
        mixed_ref[g] = (mixed / total).astype(jnp.bfloat16)
        lse_ref[g] = top + jnp.log(total)


def attend_forward(query, keyval):
    blocks, token_positions = keyval.shape[0], keyval.shape[-1]
    head_block = (GROUP, HEAD_WIDTH, token_positions)
    key_block = (blocks, 1, 1, HEAD_WIDTH, token_positions)
    area = QUERY_HEADS * token_positions * token_positions * blocks
    return pl.pallas_call(
        forward_kernel,
        grid=(KEYVAL_HEADS,),
        in_specs=[
            pl.BlockSpec(head_block, lambda j: (j, 0, 0)),
            pl.BlockSpec(key_block, lambda j: (0, 0, j, 0, 0)),
            pl.BlockSpec(key_block, lambda j: (0, 1, j, 0, 0)),
        ],
        out_specs=[
            pl.BlockSpec(head_block, lambda j: (j, 0, 0)),
            pl.BlockSpec((GROUP, 1, token_positions), lambda j: (j, 0, 0)),
        ],
        out_shape=[
            jax.ShapeDtypeStruct(query.shape, jnp.bfloat16),
            jax.ShapeDtypeStruct((QUERY_HEADS, 1, token_positions), jnp.float32),
        ],
        compiler_params=pltpu.CompilerParams(vmem_limit_bytes=VMEM_LIMIT),
        cost_estimate=pl.CostEstimate(
            flops=16 * HEAD_WIDTH * area, bytes_accessed=6 * query.size, transcendentals=area
        ),
        name="attend_forward",
    )(query, keyval, keyval)


def backward_kernel(
    query_ref, key_ref, value_ref, back_ref, mixed_ref, lse_ref, cosine_ref, sine_ref,
    back_query_ref, back_keyval_ref,
):
    place = lax.axis_index("ctx")
    blocks = key_ref.shape[0]
    queries = [query_ref[g] * jnp.bfloat16(SCALE) for g in range(GROUP)]
    backs = [back_ref[g] for g in range(GROUP)]
    tops = [lse_ref[g] for g in range(GROUP)]
    sums = [
        jnp.sum(backs[g].astype(jnp.float32) * mixed_ref[g].astype(jnp.float32), 0, keepdims=True)
        for g in range(GROUP)
    ]

    def step(block, carried, masked=False):
        keys = key_ref[block, 0, 0]
        keys_turned = keys.T
        values_turned = value_ref[block, 0, 0].T
        back_key = jnp.zeros(keys.shape, jnp.float32)
        back_value = jnp.zeros(keys.shape, jnp.float32)
        later = []
        for g in range(GROUP):
            scores = dot(keys_turned, queries[g], 1, 0)
            if masked:
                scores = causal(scores)
            weights = jnp.exp(scores - tops[g])
            back_weights = dot(values_turned, backs[g], 1, 0)
            back_scores = (weights * (back_weights - sums[g])).astype(jnp.bfloat16)
            later.append(carried[g] + dot(keys, back_scores, 1, 0))
            back_key += dot(queries[g], back_scores, 1, 1)
            back_value += dot(backs[g], weights.astype(jnp.bfloat16), 1, 1)
        back_keyval_ref[block, 0, 0] = back_key.astype(jnp.bfloat16)
        back_keyval_ref[block, 1, 0] = back_value.astype(jnp.bfloat16)
        return tuple(later)

    start = tuple(jnp.zeros(query_ref.shape[1:], jnp.float32) for g in range(GROUP))
    carried = lax.fori_loop(0, place, step, step(place, start, True))

    def clear(block, unused):
        zero = jnp.zeros(key_ref.shape[3:], jnp.bfloat16)
        back_keyval_ref[block, 0, 0] = zero
        back_keyval_ref[block, 1, 0] = zero
        return unused

    lax.fori_loop(place + 1, blocks, clear, 0)
    cosine = cosine_ref[...]
    sine = sine_ref[...]
    for g in range(GROUP):
        leading = carried[g][:HALF] * SCALE
        trailing = carried[g][HALF:] * SCALE
        back_query_ref[g, :HALF] = (leading * cosine + trailing * sine).astype(jnp.bfloat16)
        back_query_ref[g, HALF:] = (trailing * cosine - leading * sine).astype(jnp.bfloat16)


def attend_backward(query, keyval, back_mixed, mixed, lse, cosine, sine, first, count):
    blocks, token_positions = keyval.shape[0], keyval.shape[-1]
    head_block = (GROUP, HEAD_WIDTH, token_positions)
    key_block = (blocks, 1, 1, HEAD_WIDTH, token_positions)
    area = count * GROUP * token_positions * token_positions * blocks
    heads = pl.BlockSpec(head_block, lambda j: (j + first, 0, 0))
    table = pl.BlockSpec((HALF, token_positions), lambda j: (0, 0))
    return pl.pallas_call(
        backward_kernel,
        grid=(count,),
        in_specs=[
            heads,
            pl.BlockSpec(key_block, lambda j: (0, 0, j + first, 0, 0)),
            pl.BlockSpec(key_block, lambda j: (0, 1, j + first, 0, 0)),
            heads,
            heads,
            pl.BlockSpec((GROUP, 1, token_positions), lambda j: (j + first, 0, 0)),
            table,
            table,
        ],
        out_specs=[
            pl.BlockSpec(head_block, lambda j: (j, 0, 0)),
            pl.BlockSpec((blocks, 2, 1, HEAD_WIDTH, token_positions), lambda j: (0, 0, j, 0, 0)),
        ],
        out_shape=[
            jax.ShapeDtypeStruct((count * GROUP, HEAD_WIDTH, token_positions), jnp.bfloat16),
            jax.ShapeDtypeStruct(
                (blocks, 2, count, HEAD_WIDTH, token_positions), jnp.bfloat16
            ),
        ],
        compiler_params=pltpu.CompilerParams(vmem_limit_bytes=VMEM_LIMIT),
        cost_estimate=pl.CostEstimate(
            flops=40 * HEAD_WIDTH * area, bytes_accessed=10 * query.size, transcendentals=area
        ),
        name="attend_backward",
    )(query, keyval, keyval, back_mixed, mixed, lse, cosine, sine)


def on_device(
    tokens, cotangent, input_gain, w_query, w_keyval, w_output, middle_gain, w_gate, w_up, w_down
):
    half = lax.axis_index("tp")
    low_half = half == 0
    pair = [(0, 1), (1, 0)]

    def to_partner(value_rows):
        return lax.ppermute(value_rows, "tp", pair)

    def in_order(mine, received):
        return jnp.concatenate(
            [jnp.where(low_half, mine, received), jnp.where(low_half, received, mine)], 0
        )

    def take(value_rows, index):
        return lax.dynamic_index_in_dim(value_rows, index, 0, keepdims=False)

    tokens_own = in_order(take(tokens, half), to_partner(take(tokens, 1 - half)))
    full_gain_one, full_gain_two = (
        lax.all_gather(input_gain, "fsdp", axis=0, tiled=True),
        lax.all_gather(middle_gain, "fsdp", axis=0, tiled=True),
    )
    full_in = lax.all_gather(jnp.concatenate([w_query, w_keyval], 1), "fsdp", axis=0, tiled=True)
    full_output = lax.all_gather(w_output, "fsdp", axis=0, tiled=True)
    full_gate = lax.all_gather(w_gate, "fsdp", axis=0, tiled=True)
    full_up = lax.all_gather(w_up, "fsdp", axis=0, tiled=True)
    full_down = lax.all_gather(w_down, "fsdp", axis=0, tiled=True)
    cotangent_received = to_partner(cotangent)
    cotangent_own = in_order(take(cotangent, half), take(cotangent_received, half))
    cotangent_other = in_order(take(cotangent, 1 - half), take(cotangent_received, 1 - half))

    token_positions = tokens_own.shape[0]
    cosine, sine = rope_tables(token_positions, lax.axis_index("ctx") * token_positions)
    gain_one = full_gain_one.astype(jnp.float32)
    inputs = tokens_own.astype(jnp.float32)
    unit_one, inverse_one = normalize(inputs)
    normed_one = (unit_one * gain_one).astype(jnp.bfloat16)
    keyval_raw = dot(full_in[:, QUERY_WIDTH:], normed_one, 0, 1)
    keyval_low = jnp.concatenate(
        [apply_rotary(keyval_raw[:KEY_WIDTH], cosine, sine), keyval_raw[KEY_WIDTH:]], 0
    ).astype(jnp.bfloat16)
    keyval = lax.all_gather(keyval_low, "ctx", axis=0, tiled=False)
    keyval = keyval.reshape(keyval.shape[0], 2, KEYVAL_HEADS, HEAD_WIDTH, token_positions)
    query_raw = dot(full_in[:, :QUERY_WIDTH], normed_one, 0, 1)
    query_low = (
        apply_rotary(query_raw, cosine, sine)
        .astype(jnp.bfloat16)
        .reshape(QUERY_HEADS, HEAD_WIDTH, token_positions)
    )
    mixed_heads, lse = attend_forward(query_low, keyval)
    mixed_low = mixed_heads.reshape(QUERY_WIDTH, token_positions)
    middle = inputs + dot(mixed_low, full_output, 0, 0)

    gain_two = full_gain_two.astype(jnp.float32)
    unit_two, inverse_two = normalize(middle)
    normed_two = (unit_two * gain_two).astype(jnp.bfloat16)
    normed_other = to_partner(normed_two)

    def feed(rows, back_rows):
        gate_proj = dot(rows, full_gate, 1, 0)
        up_proj = dot(rows, full_up, 1, 0)
        sigmoid_gate = jax.nn.sigmoid(gate_proj)
        swish_gate = gate_proj * sigmoid_gate
        hidden = (swish_gate * up_proj).astype(jnp.bfloat16)
        back_hidden = dot(back_rows, full_down, 1, 0)
        back_gate = (
            back_hidden * up_proj * sigmoid_gate * (1.0 + gate_proj * (1.0 - sigmoid_gate))
        ).astype(jnp.bfloat16)
        back_up = (back_hidden * swish_gate).astype(jnp.bfloat16)
        return (hidden, back_gate, back_up)

    def feed_input_back(back_gate, back_up):
        return dot(back_gate, full_gate, 1, 1) + dot(back_up, full_up, 1, 1)

    hidden_own, back_gate_own, back_up_own = feed(normed_two, cotangent_own)
    hidden_other, back_gate_other, back_up_other = feed(normed_other, cotangent_other)
    back_two_received = to_partner(
        feed_input_back(back_gate_other, back_up_other).astype(jnp.bfloat16)
    )
    back_two = feed_input_back(back_gate_own, back_up_own) + back_two_received.astype(jnp.float32)
    feed_received = to_partner(dot(hidden_other, full_down, 1, 1).astype(jnp.bfloat16))
    result_own = (
        middle + dot(hidden_own, full_down, 1, 1) + feed_received.astype(jnp.float32)
    ).astype(jnp.bfloat16)

    def feed_gradient(left_own, right_own, left_other, right_other):
        gradient = dot(left_own, right_own, 0, 0) + dot(left_other, right_other, 0, 0)
        shared = lax.psum_scatter(
            gradient.astype(jnp.bfloat16), "fsdp", scatter_dimension=0, tiled=True
        )
        return lax.psum(shared, "ctx").astype(jnp.float32)

    share_down = feed_gradient(cotangent_own, hidden_own, cotangent_other, hidden_other)
    share_gate = feed_gradient(normed_two, back_gate_own, normed_other, back_gate_other)
    share_up = feed_gradient(normed_two, back_up_own, normed_other, back_up_other)

    grad_gain_two = jnp.sum(back_two * unit_two, axis=0)
    back_middle = cotangent_own.astype(jnp.float32) + norm_back(
        back_two * gain_two, unit_two, inverse_two
    )
    back_attention = back_middle.astype(jnp.bfloat16)
    back_mixed = dot(full_output, back_attention, 1, 1).astype(jnp.bfloat16)
    back_mixed = back_mixed.reshape(query_low.shape)
    grad_output = dot(mixed_low, back_attention, 1, 0).astype(jnp.bfloat16)
    share_output = lax.psum(
        lax.psum_scatter(grad_output, "fsdp", scatter_dimension=0, tiled=True), ("ctx", "tp")
    ).astype(jnp.float32)

    back_query = []
    back_key = []
    back_value = []
    for first, count in ((0, 3), (3, 2)):
        part_query, part_keyval = attend_backward(
            query_low, keyval, back_mixed, mixed_heads, lse, cosine, sine, first, count
        )
        owned = lax.psum_scatter(
            part_keyval.reshape(keyval.shape[0], 2 * count * HEAD_WIDTH, token_positions),
            "ctx",
            scatter_dimension=0,
            tiled=False,
        ).astype(jnp.float32)
        back_query.append(part_query.reshape(-1, token_positions))
        back_key.append(
            apply_rotary(owned[: count * HEAD_WIDTH], cosine, -sine).astype(jnp.bfloat16)
        )
        back_value.append(owned[count * HEAD_WIDTH :].astype(jnp.bfloat16))
    back_in = jnp.concatenate(back_query + back_key + back_value, 0)
    grad_in = dot(normed_one, back_in, 0, 1)
    back_one = dot(back_in, full_in, 0, 1)
    grad_gain_one = jnp.sum(back_one * unit_one, axis=0)
    back_inputs = back_middle + norm_back(back_one * gain_one, unit_one, inverse_one)

    def to_positions(value_rows):
        split = value_rows.reshape(2, token_positions // 2, value_rows.shape[-1])
        received = to_partner(take(split, 1 - half))
        return in_order(take(split, half)[None], received[None])

    result = to_positions(result_own)
    grad_tokens = to_positions(back_inputs.astype(jnp.bfloat16)).astype(jnp.float32)
    gradients = jnp.concatenate([grad_in, grad_gain_one[:, None], grad_gain_two[:, None]], 1)
    share_in = lax.psum(
        lax.psum_scatter(
            gradients.astype(jnp.bfloat16), "fsdp", scatter_dimension=0, tiled=True
        ),
        ("ctx", "tp"),
    ).astype(jnp.float32)
    width = full_in.shape[1]
    return (
        result,
        grad_tokens,
        share_in[:, width],
        share_in[:, :QUERY_WIDTH],
        share_in[:, QUERY_WIDTH:width],
        share_output,
        share_in[:, width + 1],
        share_gate,
        share_up,
        share_down,
    )


def solution(mesh):
    rows = P("fsdp", ("ctx", "tp"), None)
    specs = (
        P("fsdp"), P("fsdp", None), P("fsdp", None), P("fsdp", None),
        P("fsdp"), P("fsdp", "tp"), P("fsdp", "tp"), P("fsdp", "tp"),
    )
    return jax.shard_map(
        on_device,
        mesh=mesh,
        in_specs=(rows, rows) + specs,
        out_specs=(rows, rows) + specs,
        check_vma=False,
    )
```

time: 1060 us -> 700 us (0.66)
  matrix products: 260 us -> 88.7 us
  waiting for transfers between devices: 568 us -> 485 us
  local copies, waits for them, and re-layouts: 112 us -> 40.5 us
  other arithmetic: 60.4 us -> 21.7 us
  blocking collectives: 35.6 us -> 6.6 us
  Pallas kernels: 0 us -> 22.7 us
  starting transfers between devices: 1.43 us -> 13.1 us
    dot_general x88 -> x25, matrix products: 260 us -> 88.7 us  [dot(): lax.dot_general(left, right, (((left_dim,), (right_dim,)), ((), ())), pre...]
    reduce_scatter x6 -> x7, waiting for transfers between devices: 253 us -> 176 us  [the longest x3 79.8 us: feed_gradient(): lax.psum_scatter(gradient.astype(jnp.bfloat16), 'fsdp', scatter_dimension...]
    while x113 -> x0, local copies, waits for them, and re-layouts: 30.7 us -> none
    ppermute x0 -> x7, waiting for transfers between devices: none -> 29.9 us  [to_partner(): return lax.ppermute(value_rows, 'tp', pair)]
    reduce_sum x11 -> x0, other arithmetic: 24 us -> none  [the longest x10 21.3 us: head_forward(): row_total = jnp.sum(lifted, -1, keepdims=True)]
    all_gather x9 -> x6, waiting for transfers between devices: 152 us -> 129 us  [the longest x1 48.1 us: on_device(): keyval = lax.all_gather(keyval_low, 'ctx', axis=0, tiled=False)]
    pallas_call x0 -> x3, Pallas kernels: none -> 22.7 us  [the longest x2 15 us: attend_backward(): pl.pallas_call(backward_kernel, grid=(count,), in_specs=[heads, pl.BlockS...]
    psum x1 -> x0, blocking collectives: 21.5 us -> none  [on_device(): lax.psum(grad_gain_one.astype(jnp.bfloat16), ('ctx', 'tp'))]
  transfers between devices with their start and end apart: 17 -> 22, of which waited for: 13 -> 18; matrix products, arithmetic and copies ran while one was open for 19% -> 16% of each run, Pallas kernels for 0% -> 2%
where the time goes in v1:
time: 700 us; the launch traced here: 694 us
  waiting for transfers between devices  485 us (69%)
  matrix products  88.7 us (13%)
  local copies, waits for them, and re-layouts  40.5 us (6%)
  Pallas kernels  22.7 us (3%)
  other arithmetic  21.7 us (3%)
  between operations  15.7 us (2%)
  starting transfers between devices  13.1 us (2%)
    dot_general x25, matrix products, dot(): lax.dot_general(left, right, (((left_dim,), (right_dim,)), ((), ())), pre...  88.7 us
    psum x1, waiting for transfers between devices, on_device(): lax.psum(lax.psum_scatter(gradients.astype(jnp.bfloat16), 'fsdp', scatter...  81.5 us
    reduce_scatter x3, waiting for transfers between devices, feed_gradient(): lax.psum_scatter(gradient.astype(jnp.bfloat16), 'fsdp', scatter_dimension...  79.8 us
    psum x1, waiting for transfers between devices, feed_gradient(): return lax.psum(shared, 'ctx').astype(jnp.float32)  67 us
    all_gather x1, waiting for transfers between devices, on_device(): keyval = lax.all_gather(keyval_low, 'ctx', axis=0, tiled=False)  48.1 us
    reduce_scatter x2, waiting for transfers between devices, on_device(): lax.psum_scatter(part_keyval.reshape(keyval.shape[0], 2 * count * HEAD_WI...  42.5 us
    reduce_scatter x1, waiting for transfers between devices, on_device(): lax.psum_scatter(gradients.astype(jnp.bfloat16), 'fsdp', scatter_dimensio...  41 us
    ppermute x7, waiting for transfers between devices, to_partner(): return lax.ppermute(value_rows, 'tp', pair)  29.9 us
  transfers between devices with their start and end apart: 22, of which 18 were waited for; matrix products, arithmetic and copies ran while one was open for 16% of the time, Pallas kernels for 2%

profile of v1, /device:TPU:0, one launch (start us, length us, event | category | flops | bytes accessed | tf_op | source)
XLA Modules:
  0.0 694.4 jit_solution(291116607191623145)
XLA Ops:
  14.4 6.6 all-reduce.4
  24.3 17.5 %all-gather.7.cloned.1.call-done = bf16[960,1600]{1,0:T(8,128)(2,1)} async-done(((bf16[240,1600]{1,0:T(8,128)(2,1)}), bf16[960,1600]{1,0:T(8,128)(2,1)}) %all-gather.7.cloned.1.call-update) | async-done | bytes 3072016 | tf_op jit(solution)/shard_map/all_gather | solution.py:249
  52.7 48.1 %all-gather.9.cloned.1.call-done = bf16[4,640,512]{2,1,0:T(8,128)(2,1)} async-done(((bf16[1,640,512]{2,1,0:T(8,128)(2,1)}), bf16[4,640,512]{2,1,0:T(8,128)(2,1)}) %all-gather.9.cloned.1.call-update) | async-done | bytes 2621456 | tf_op jit(solution)/shard_map/all_gather | solution.py:268
  102.5 7.7 %attend_forward.1 = (bf16[15,64,512]{2,1,0:T(8,128)(2,1)S(1)}, f32[15,1,512]{2,1,0:T(1,128)S(1)}) custom-call(bf16[15,64,512]{2,1,0:T(8,128)(2,1)S(1)} %bitcast.98, bf16[4,2,5,64,512]{4,3,2,1,0:T(8,128)(2,1)S(1)} %bitcast.103, bf16[4,2,5,64,512]{4,3,2,1,0:T(8,128)(2,1)S(1)} %bitcast.104), custom_call_target="tpu_custom_call" | custom-call | flops 16106127360 | bytes 2949120 | tf_op jit(solution)/shard_map/attend_forward/pallas_call | solution.py:110
  110.3 12.8 %all-gather.11.cloned.1.call-done = bf16[960,960]{1,0:T(8,128)(2,1)} async-done(((bf16[240,960]{1,0:T(8,128)(2,1)}), bf16[960,960]{1,0:T(8,128)(2,1)}) %all-gather.11.cloned.1.call-update) | async-done | bytes 1843216 | tf_op jit(solution)/shard_map/all_gather | solution.py:250
  131.8 17.3 %all-gather.13.cloned.1.call-done = bf16[960,1280]{1,0:T(8,128)(2,1)} async-done(((bf16[240,1280]{1,0:T(8,128)(2,1)}), bf16[960,1280]{1,0:T(8,128)(2,1)}) %all-gather.13.cloned.1.call-update) | async-done | bytes 2457616 | tf_op jit(solution)/shard_map/all_gather | solution.py:251
  153.9 21.3 %all-gather.15.cloned.1.call-done = bf16[960,1280]{1,0:T(8,128)(2,1)} async-done(((bf16[240,1280]{1,0:T(8,128)(2,1)}), bf16[960,1280]{1,0:T(8,128)(2,1)}) %all-gather.15.cloned.1.call-update) | async-done | bytes 2457616 | tf_op jit(solution)/shard_map/all_gather | solution.py:252
  188.9 12.4 %all-gather.17.cloned.1.call-done = bf16[960,1280]{1,0:T(8,128)(2,1)} async-done(((bf16[240,1280]{1,0:T(8,128)(2,1)}), bf16[960,1280]{1,0:T(8,128)(2,1)}) %all-gather.17.cloned.1.call-update) | async-done | bytes 2457616 | tf_op jit(solution)/shard_map/all_gather | solution.py:253
  201.3 6.2 multiply_convert_fusion
  218.7 17.0 %collective-permute-done.5 = bf16[512,960]{0,1:T(8,128)(2,1)S(1)} collective-permute-done((bf16[512,960]{0,1:T(8,128)(2,1)S(1)}, bf16[512,960]{0,1:T(8,128)(2,1)S(1)}, u32[]{:S(2)}, u32[]{:S(2)}) %collective-permute-start.5) | collective-permute-done | bytes 983072 | tf_op jit(solution)/shard_map/ppermute | solution.py:234
  241.9 6.1 attend_backward.3
  251.0 8.9 %attend_backward.2 = (bf16[9,64,512]{2,1,0:T(8,128)(2,1)S(1)}, bf16[4,2,3,64,512]{4,3,2,1,0:T(8,128)(2,1)}) custom-call(bf16[15,64,512]{2,1,0:T(8,128)(2,1)S(1)} %bitcast.100, bf16[4,2,5,64,512]{4,3,2,1,0:T(8,128)(2,1)S(1)} %bitcast.107, bf16[4,2,5,64,512]{4,3,2,1,0:T(8,128)(2,1)S(1)} %bitcast.108, bf16[15,64,512]{2,1,0:T(8,128)(2,1)S(1)} %bitcast.112, ...), custom_call_target="tpu_custom_call" | custom-call | flops 24159191040 | bytes 4915200 | tf_op jit(solution)/shard_map/attend_backward/pallas_call | solution.py:195
  291.3 41.2 %reduce-scatter.8.cloned.1.call-done = bf16[1,384,512]{2,1,0:T(8,128)(2,1)} async-done(((bf16[4,384,512]{2,1,0:T(8,128)(2,1)}), bf16[1,384,512]{2,1,0:T(8,128)(2,1)}) %reduce-scatter.8.cloned.1.call-update) | async-done | bytes 393232 | tf_op jit(solution)/shard_map/reduce_scatter | solution.py:342
  337.2 5.9 fusion.12
  343.3 5.2 convolution_convert_fusion
  348.5 6.0 concatenate.50
  360.7 7.2 %reduce-scatter.16.cloned.1.call-done = bf16[240,1280]{1,0:T(8,128)(2,1)} async-done(((bf16[960,1280]{1,0:T(8,128)(2,1)}), bf16[240,1280]{1,0:T(8,128)(2,1)}) %reduce-scatter.16.cloned.1.call-update) | async-done | bytes 614416 | tf_op jit(solution)/shard_map/reduce_scatter | solution.py:314
  367.9 36.1 %reduce-scatter.18.cloned.1.call-done = bf16[240,1280]{1,0:T(8,128)(2,1)} async-done(((bf16[960,1280]{1,0:T(8,128)(2,1)}), bf16[240,1280]{1,0:T(8,128)(2,1)}) %reduce-scatter.18.cloned.1.call-update) | async-done | bytes 614416 | tf_op jit(solution)/shard_map/reduce_scatter | solution.py:314
  404.0 36.5 %reduce-scatter.20.cloned.1.call-done = bf16[240,1280]{1,0:T(8,128)(2,1)} async-done(((bf16[960,1280]{1,0:T(8,128)(2,1)}), bf16[240,1280]{1,0:T(8,128)(2,1)}) %reduce-scatter.20.cloned.1.call-update) | async-done | bytes 614416 | tf_op jit(solution)/shard_map/reduce_scatter | solution.py:314
  461.0 12.5 %reduce-scatter.14.cloned.1.call-done = bf16[240,960]{1,0:T(8,128)(2,1)} async-done(((bf16[960,960]{1,0:T(8,128)(2,1)}), bf16[240,960]{1,0:T(8,128)(2,1)}) %reduce-scatter.14.cloned.1.call-update) | async-done | bytes 460816 | tf_op jit(solution)/shard_map/reduce_scatter | solution.py:332
  473.5 41.0 %reduce-scatter.12.cloned.1.call-done = bf16[240,1602]{1,0:T(8,128)(2,1)} async-done(((bf16[960,1602]{1,0:T(8,128)(2,1)}), bf16[240,1602]{1,0:T(8,128)(2,1)}) %reduce-scatter.12.cloned.1.call-update) | async-done | bytes 768976 | tf_op jit(solution)/shard_map/reduce_scatter | solution.py:368
  517.3 10.3 %collective-permute-done.6 = bf16[256,960]{0,1:T(8,128)(2,1)S(1)} collective-permute-done((bf16[256,960]{0,1:T(8,128)(2,1)S(1)}, bf16[256,960]{0,1:T(8,128)(2,1)S(1)}, u32[]{:S(2)}, u32[]{:S(2)}) %collective-permute-start.6) | collective-permute-done | bytes 491552 | tf_op jit(solution)/shard_map/ppermute | solution.py:234
  529.1 67.0 %all-reduce.10.cloned.1.call-done = (bf16[240,1280]{1,0:T(8,128)(2,1)}, bf16[240,1280]{1,0:T(8,128)(2,1)}, bf16[240,1280]{1,0:T(8,128)(2,1)}) async-done(((bf16[240,1280]{1,0:T(8,128)(2,1)}, bf16[240,1280]{1,0:T(8,128)(2,1)}, bf16[240,1280]{1,0:T(8,128)(2,1)}), (bf16[240,1280]{1,0:T(8,128)(2,1)}, bf16[240,1280]{1,0:T(8,128)(2,1)}, bf16[240,1280]{1,0:T(8,128)(2,1)})) %all-reduce.10.cloned.1.call-update) | async-done | bytes 1843216 | tf_op jit(solution)/shard_map/psum | solution.py:317
  600.7 81.5 %all-reduce.8.cloned.1.call-done = (bf16[240,1602]{1,0:T(8,128)(2,1)}, bf16[240,960]{1,0:T(8,128)(2,1)}) async-done(((bf16[240,1602]{1,0:T(8,128)(2,1)}, bf16[240,960]{1,0:T(8,128)(2,1)}), (bf16[240,1602]{1,0:T(8,128)(2,1)}, bf16[240,960]{1,0:T(8,128)(2,1)})) %all-reduce.8.cloned.1.call-update) | async-done | bytes 1229776 | tf_op jit(solution)/shard_map/psum | solution.py:367
  (231 shorter events, 146.4 us)
Async XLA Ops:
  7.2 34.5 %all-gather.7.cloned.1.call-start = ((), (), s32[]{:S(2)}) async-start(), calls=%async_computation.7 | async-start | bytes 3993600 | tf_op jit(solution)/shard_map/all_gather | solution.py:249
  9.6 91.2 %all-gather.9.cloned.1.call-start = ((), (), s32[]{:S(2)}) async-start(), calls=%async_computation.8 | async-start | bytes 3276800 | tf_op jit(solution)/shard_map/all_gather | solution.py:268
  9.7 14.2 %collective-permute-start = (bf16[256,960]{0,1:T(8,128)(2,1)S(1)}, bf16[256,960]{0,1:T(8,128)(2,1)S(1)}, u32[]{:S(2)}, u32[]{:S(2)}) collective-permute-start(bf16[256,960]{0,1:T(8,128)(2,1)S(1)} %dynamic-slice_bitcast_fusion), channel_id=1, source_target_pairs={{0,1},{1,0},{2,3},{3,2},{4,5},{5,4},{6,7},{7,6},{8,9},{9,8},{10,11... | collective-permute-start | bytes 1474568 | tf_op jit(solution)/shard_map/ppermute | solution.py:234
  21.4 269.8 %copy-start.43 = (f32[32,512]{1,0:T(8,128)}, f32[32,512]{1,0:T(8,128)S(1)}, u32[]{:S(2)}) copy-start(f32[32,512]{1,0:T(8,128)S(1)} %get-tuple-element.63) | copy-start | bytes 196612
  24.0 99.1 %copy-start.18 = (bf16[256,960]{0,1:T(8,128)(2,1)}, bf16[256,960]{0,1:T(8,128)(2,1)S(1)}, u32[]{:S(2)}) copy-start(bf16[256,960]{0,1:T(8,128)(2,1)S(1)} %get-tuple-element.51) | copy-start | bytes 1474564
  45.8 77.2 %all-gather.11.cloned.1.call-start = ((), (), s32[]{:S(2)}) async-start(), calls=%async_computation.9 | async-start | bytes 2457600 | tf_op jit(solution)/shard_map/all_gather | solution.py:250
  46.6 102.5 %all-gather.13.cloned.1.call-start = ((), (), s32[]{:S(2)}) async-start(), calls=%async_computation.10 | async-start | bytes 3072000 | tf_op jit(solution)/shard_map/all_gather | solution.py:251
  47.1 128.0 %all-gather.15.cloned.1.call-start = ((), (), s32[]{:S(2)}) async-start(), calls=%async_computation.11 | async-start | bytes 3072000 | tf_op jit(solution)/shard_map/all_gather | solution.py:252
  47.7 153.5 %all-gather.17.cloned.1.call-start = ((), (), s32[]{:S(2)}) async-start(), calls=%async_computation.12 | async-start | bytes 3072000 | tf_op jit(solution)/shard_map/all_gather | solution.py:253
  47.8 81.2 %collective-permute-start.4 = (bf16[2,256,960]{1,2,0:T(8,128)(2,1)}, bf16[2,256,960]{1,2,0:T(8,128)(2,1)}, u32[]{:S(2)}, u32[]{:S(2)}) collective-permute-start(bf16[2,256,960]{1,2,0:T(8,128)(2,1)} %param.11), channel_id=1, source_target_pairs={{0,1},{1,0},{2,3},{3,2},{4,5},{5,4},{6,7},{7,6},{8,9},{9,8},{10,11... | collective-permute-start | bytes 2949128 | tf_op jit(solution)/shard_map/ppermute | solution.py:234
  49.3 240.9 %reduce-scatter.10.cloned.1.call-start = ((), (), s32[]{:S(2)}) async-start(), calls=%async_computation.14 | async-start | bytes 1310720 | tf_op jit(solution)/shard_map/reduce_scatter | solution.py:342
  127.4 52.6 %collective-permute-start.1 = (bf16[512,960]{0,1:T(8,128)(2,1)S(1)}, bf16[512,960]{0,1:T(8,128)(2,1)}, u32[]{:S(2)}, u32[]{:S(2)}) collective-permute-start(bf16[512,960]{0,1:T(8,128)(2,1)S(1)} %multiply_convert_fusion.6), channel_id=1, source_target_pairs={{0,1},{1,0},{2,3},{3,2},{4,5},{5,4},{6,7},{7,6},{8,9},{9,8},{10,11... | collective-permute-start | bytes 2949128 | tf_op jit(solution)/shard_map/ppermute | solution.py:234
  211.7 24.0 %collective-permute-start.5 = (bf16[512,960]{0,1:T(8,128)(2,1)S(1)}, bf16[512,960]{0,1:T(8,128)(2,1)S(1)}, u32[]{:S(2)}, u32[]{:S(2)}) collective-permute-start(bf16[512,960]{0,1:T(8,128)(2,1)S(1)} %add_convert_fusion.3), channel_id=1, source_target_pairs={{0,1},{1,0},{2,3},{3,2},{4,5},{5,4},{6,7},{7,6},{8,9},{9,8},{10,11... | collective-permute-start | bytes 2949128 | tf_op jit(solution)/shard_map/ppermute | solution.py:234
  248.0 84.5 %reduce-scatter.8.cloned.1.call-start = ((), (), s32[]{:S(2)}) async-start(), calls=%async_computation.13 | async-start | bytes 1966080 | tf_op jit(solution)/shard_map/reduce_scatter | solution.py:342
  260.0 107.9 %reduce-scatter.16.cloned.1.call-start = ((), (), s32[]{:S(2)}) async-start(), calls=%async_computation.17 | async-start | bytes 3072000 | tf_op jit(solution)/shard_map/reduce_scatter | solution.py:314
  267.4 136.5 %reduce-scatter.18.cloned.1.call-start = ((), (), s32[]{:S(2)}) async-start(), calls=%async_computation.18 | async-start | bytes 3072000 | tf_op jit(solution)/shard_map/reduce_scatter | solution.py:314
  275.6 164.8 %reduce-scatter.20.cloned.1.call-start = ((), (), s32[]{:S(2)}) async-start(), calls=%async_computation.19 | async-start | bytes 3072000 | tf_op jit(solution)/shard_map/reduce_scatter | solution.py:314
  282.7 190.8 %reduce-scatter.14.cloned.1.call-start = ((), (), s32[]{:S(2)}) async-start(), calls=%async_computation.16 | async-start | bytes 2457600 | tf_op jit(solution)/shard_map/reduce_scatter | solution.py:332
  286.8 227.7 %reduce-scatter.12.cloned.1.call-start = ((), (), s32[]{:S(2)}) async-start(), calls=%async_computation.15 | async-start | bytes 3993600 | tf_op jit(solution)/shard_map/reduce_scatter | solution.py:368
  354.6 241.6 %all-reduce.10.cloned.1.call-start = ((), (), s32[]{:S(2)}) async-start(), calls=%async_computation.21 | async-start | bytes 3686400 | tf_op jit(solution)/shard_map/psum | solution.py:317
  359.2 81.3 %collective-permute-start.2 = (bf16[512,960]{0,1:T(8,128)(2,1)}, bf16[512,960]{0,1:T(8,128)(2,1)S(1)}, u32[]{:S(2)}, u32[]{:S(2)}) collective-permute-start(bf16[512,960]{0,1:T(8,128)(2,1)} %convolution_convert_fusion.3), channel_id=1, source_target_pairs={{0,1},{1,0},{2,3},{3,2},{4,5},{5,4},{6,7},{7,6},{8,9},{9,8},{10,11... | collective-permute-start | bytes 2949128 | tf_op jit(solution)/shard_map/ppermute | solution.py:234
  440.5 241.7 %all-reduce.8.cloned.1.call-start = ((), (), s32[]{:S(2)}) async-start(), calls=%async_computation.20 | async-start | bytes 2580480 | tf_op jit(solution)/shard_map/psum | solution.py:367
  459.3 56.9 %collective-permute-start.3 = (bf16[256,960]{0,1:T(8,128)(2,1)}, bf16[256,960]{0,1:T(8,128)(2,1)S(1)}, u32[]{:S(2)}, u32[]{:S(2)}) collective-permute-start(bf16[256,960]{0,1:T(8,128)(2,1)} %bitcast.97), channel_id=1, source_target_pairs={{0,1},{1,0},{2,3},{3,2},{4,5},{5,4},{6,7},{7,6},{8,9},{9,8},{10,11... | collective-permute-start | bytes 1474568 | tf_op jit(solution)/shard_map/ppermute | solution.py:234
  514.6 13.0 %collective-permute-start.6 = (bf16[256,960]{0,1:T(8,128)(2,1)S(1)}, bf16[256,960]{0,1:T(8,128)(2,1)S(1)}, u32[]{:S(2)}, u32[]{:S(2)}) collective-permute-start(bf16[256,960]{0,1:T(8,128)(2,1)S(1)} %bitcast.120), channel_id=1, source_target_pairs={{0,1},{1,0},{2,3},{3,2},{4,5},{5,4},{6,7},{7,6},{8,9},{9,8},{10,11... | collective-permute-start | bytes 1474568 | tf_op jit(solution)/shard_map/ppermute | solution.py:234
  (50 other events, 668.0 us)
Sparse Core Ops, SparseCore 0:
  10.2 31.5 all-gather.6
  46.0 54.8 all-gather.8
  102.4 20.6 all-gather.10
  124.5 24.5 all-gather.12
  150.5 24.6 all-gather.14
  176.6 24.6 all-gather.16
  248.2 42.0 reduce-scatter.9
  292.6 39.8 reduce-scatter.7
  335.2 32.6 reduce-scatter.15
  370.3 33.6 reduce-scatter.17
  406.7 33.6 reduce-scatter.19
  442.9 30.6 reduce-scatter.13
  476.2 38.2 reduce-scatter.11
  517.0 79.1 all-reduce.9
  599.6 82.5 all-reduce.7

commit v2 on v1

--- a/solution.py
+++ b/solution.py
@@ -67,8 +67,8 @@
         return causal(scores) if masked else scores
 
     def first():
-        keys_turned = key_ref[place, 0, 0].T
-        values = value_ref[place, 0, 0]
+        keys_turned = key_ref[0, 0, 0].T
+        values = value_ref[0, 0, 0]
         carried = []
         for g in range(GROUP):
             scores = scores_of(keys_turned, g, True)
@@ -95,7 +95,7 @@
             ]
         return tuple(later)
 
-    carried = lax.fori_loop(0, place, step, first())
+    carried = lax.fori_loop(1, place + 1, step, first())
     for g in range(GROUP):
         top, total, mixed = carried[3 * g : 3 * g + 3]
         mixed_ref[g] = (mixed / total).astype(jnp.bfloat16)
@@ -167,7 +167,7 @@
         return tuple(later)
 
     start = tuple(jnp.zeros(query_ref.shape[1:], jnp.float32) for g in range(GROUP))
-    carried = lax.fori_loop(0, place, step, step(place, start, True))
+    carried = lax.fori_loop(1, place + 1, step, step(0, start, True))
 
     def clear(block, unused):
         zero = jnp.zeros(key_ref.shape[3:], jnp.bfloat16)
@@ -223,6 +223,54 @@
     )(query, keyval, keyval, back_mixed, mixed, lse, cosine, sine)
 
 
+def move_along(value, distance):
+    blocks = lax.axis_size("ctx")
+    pairs = [(i, i + distance) for i in range(blocks) if 0 <= i + distance < blocks]
+    return lax.ppermute(value, "ctx", pairs)
+
+
+def trade(value, axis, step):
+    pairs = [(i, i ^ step) for i in range(lax.axis_size(axis))]
+    return lax.ppermute(value, axis, pairs)
+
+
+def add_low(left, right):
+    return (left.astype(jnp.float32) + right.astype(jnp.float32)).astype(jnp.bfloat16)
+
+
+def scatter_sum(value, axis):
+    size = lax.axis_size(axis)
+    index = lax.axis_index(axis)
+    rows = value.shape[0] // size
+    step = 1
+    while step < size:
+        count = value.shape[0] // (2 * rows)
+        split = value.reshape(count, 2, rows, value.shape[-1])
+        second = (index // step) % 2 == 1
+        kept = jnp.where(second, split[:, 1], split[:, 0])
+        sent = jnp.where(second, split[:, 0], split[:, 1])
+        value = add_low(kept, trade(sent, axis, step)).reshape(count * rows, value.shape[-1])
+        step *= 2
+    return value
+
+
+def whole_sum(value, others):
+    half_rows = value.shape[0] // 2
+    second = lax.axis_index("ctx") % 2 == 1
+    upper, lower = value[:half_rows], value[half_rows:]
+    received = trade(jnp.where(second, upper, lower), "ctx", 1)
+    total = add_low(jnp.where(second, lower, upper), received)
+    for axis, first_step in others:
+        step = first_step
+        while step < lax.axis_size(axis):
+            total = add_low(total, trade(total, axis, step))
+            step *= 2
+    received = trade(total, "ctx", 1)
+    return jnp.concatenate(
+        [jnp.where(second, received, total), jnp.where(second, total, received)], 0
+    ).astype(jnp.float32)
+
+
 def on_device(
     tokens, cotangent, input_gain, w_query, w_keyval, w_output, middle_gain, w_gate, w_up, w_down
 ):
@@ -265,8 +313,9 @@
     keyval_low = jnp.concatenate(
         [apply_rotary(keyval_raw[:KEY_WIDTH], cosine, sine), keyval_raw[KEY_WIDTH:]], 0
     ).astype(jnp.bfloat16)
-    keyval = lax.all_gather(keyval_low, "ctx", axis=0, tiled=False)
-    keyval = keyval.reshape(keyval.shape[0], 2, KEYVAL_HEADS, HEAD_WIDTH, token_positions)
+    blocks = lax.axis_size("ctx")
+    keyval = jnp.stack([keyval_low] + [move_along(keyval_low, s) for s in range(1, blocks)], 0)
+    keyval = keyval.reshape(blocks, 2, KEYVAL_HEADS, HEAD_WIDTH, token_positions)
     query_raw = dot(full_in[:, :QUERY_WIDTH], normed_one, 0, 1)
     query_low = (
         apply_rotary(query_raw, cosine, sine)
@@ -311,10 +360,8 @@
 
     def feed_gradient(left_own, right_own, left_other, right_other):
         gradient = dot(left_own, right_own, 0, 0) + dot(left_other, right_other, 0, 0)
-        shared = lax.psum_scatter(
-            gradient.astype(jnp.bfloat16), "fsdp", scatter_dimension=0, tiled=True
-        )
-        return lax.psum(shared, "ctx").astype(jnp.float32)
+        shared = scatter_sum(gradient.astype(jnp.bfloat16), "fsdp")
+        return whole_sum(shared, (("ctx", 2),))
 
     share_down = feed_gradient(cotangent_own, hidden_own, cotangent_other, hidden_other)
     share_gate = feed_gradient(normed_two, back_gate_own, normed_other, back_gate_other)
@@ -328,9 +375,7 @@
     back_mixed = dot(full_output, back_attention, 1, 1).astype(jnp.bfloat16)
     back_mixed = back_mixed.reshape(query_low.shape)
     grad_output = dot(mixed_low, back_attention, 1, 0).astype(jnp.bfloat16)
-    share_output = lax.psum(
-        lax.psum_scatter(grad_output, "fsdp", scatter_dimension=0, tiled=True), ("ctx", "tp")
-    ).astype(jnp.float32)
+    share_output = whole_sum(scatter_sum(grad_output, "fsdp"), (("tp", 1), ("ctx", 2)))
 
     back_query = []
     back_key = []
@@ -339,12 +384,10 @@
         part_query, part_keyval = attend_backward(
             query_low, keyval, back_mixed, mixed_heads, lse, cosine, sine, first, count
         )
-        owned = lax.psum_scatter(
-            part_keyval.reshape(keyval.shape[0], 2 * count * HEAD_WIDTH, token_positions),
-            "ctx",
-            scatter_dimension=0,
-            tiled=False,
-        ).astype(jnp.float32)
+        part_keyval = part_keyval.reshape(blocks, 2 * count * HEAD_WIDTH, token_positions)
+        owned = part_keyval[0].astype(jnp.float32)
+        for s in range(1, blocks):
+            owned += move_along(part_keyval[s], -s).astype(jnp.float32)
         back_query.append(part_query.reshape(-1, token_positions))
         back_key.append(
             apply_rotary(owned[: count * HEAD_WIDTH], cosine, -sine).astype(jnp.bfloat16)

time: 700 us -> 530 us (0.76)
  waiting for transfers between devices: 485 us -> 284 us
  starting transfers between devices: 13.1 us -> 48 us
  other arithmetic: 21.7 us -> 42.6 us
  matrix products: 88.7 us -> 68.5 us
    ppermute x0 -> x30, waiting for transfers between devices: none -> 187 us  [the longest x9 99 us: move_along(): return lax.ppermute(value, 'ctx', pairs)]
    reduce_scatter x6 -> x0, waiting for transfers between devices: 135 us -> none  [the longest x3 79.8 us: feed_gradient(): lax.psum_scatter(gradient.astype(jnp.bfloat16), 'fsdp', scatter_dimension...]
    psum x1 -> x0, waiting for transfers between devices: 67 us -> none  [feed_gradient(): return lax.psum(shared, 'ctx').astype(jnp.float32)]
    all_gather x1 -> x0, waiting for transfers between devices: 48.1 us -> none  [on_device(): keyval = lax.all_gather(keyval_low, 'ctx', axis=0, tiled=False)]
    reduce_scatter x1, waiting for transfers between devices: 41 us -> 0.01 us  [on_device(): lax.psum_scatter(gradients.astype(jnp.bfloat16), 'fsdp', scatter_dimensio...]
    ppermute x0 -> x30, starting transfers between devices: none -> 38.9 us  [the longest x21 20.9 us: trade(): return lax.ppermute(value, axis, pairs)]
    psum x1, waiting for transfers between devices: 81.5 us -> 48.5 us  [on_device(): lax.psum(lax.psum_scatter(gradients.astype(jnp.bfloat16), 'fsdp', scatter...]
    all_gather x1, waiting for transfers between devices: 21.3 us -> 0.01 us  [on_device(): full_up = lax.all_gather(w_up, 'fsdp', axis=0, tiled=True)]
  transfers between devices with their start and end apart: 22 -> 44, of which waited for: 18 -> 22; matrix products, arithmetic and copies ran while one was open for 16% -> 23% of each run, Pallas kernels for 2% -> 4%
where the time goes in v2:
time: 530 us; the launch traced here: 522 us
  waiting for transfers between devices  284 us (54%)
  matrix products  68.5 us (13%)
  starting transfers between devices  48 us (9%)
  other arithmetic  42.6 us (8%)
  local copies, waits for them, and re-layouts  34.1 us (6%)
  Pallas kernels  21.2 us (4%)
  between operations  16.3 us (3%)
  blocking collectives  6.88 us (1%)
    ppermute x9, waiting for transfers between devices, move_along(): return lax.ppermute(value, 'ctx', pairs)  99 us
    ppermute x21, waiting for transfers between devices, trade(): return lax.ppermute(value, axis, pairs)  88.4 us
    dot_general x25, matrix products, dot(): lax.dot_general(left, right, (((left_dim,), (right_dim,)), ((), ())), pre...  68.5 us
    psum x1, waiting for transfers between devices, on_device(): lax.psum(lax.psum_scatter(gradients.astype(jnp.bfloat16), 'fsdp', scatter...  48.5 us
    ppermute x7, waiting for transfers between devices, to_partner(): return lax.ppermute(value_rows, 'tp', pair)  29.2 us
    ppermute x21, starting transfers between devices, trade(): return lax.ppermute(value, axis, pairs)  20.9 us
    ppermute x9, starting transfers between devices, move_along(): return lax.ppermute(value, 'ctx', pairs)  18.1 us
    all_gather x1, waiting for transfers between devices, on_device(): full_down = lax.all_gather(w_down, 'fsdp', axis=0, tiled=True)  17.3 us
  transfers between devices with their start and end apart: 44, of which 22 were waited for; matrix products, arithmetic and copies ran while one was open for 23% of the time, Pallas kernels for 4%

profile of v2, /device:TPU:0, one launch (start us, length us, event | category | flops | bytes accessed | tf_op | source)
XLA Modules:
  0.0 522.0 jit_solution(15918234388384990716)
XLA Ops:
  16.7 6.9 %all-reduce.2 = (bf16[960]{0:T(1024)(128)(2,1)S(1)}, bf16[960]{0:T(1024)(128)(2,1)S(1)}) all-reduce(bf16[960]{0:T(1024)(128)(2,1)S(1)} %dynamic-update-slice, bf16[960]{0:T(1024)(128)(2,1)S(1)} %dynamic-update-slice.1), channel_id=1, replica_groups=mesh['fsdp'=4,'ctx'=4,'tp'=2] {'fsdp'}, use_global_device_ids=true, to_apply=%add | all-reduce | flops 1920 | bytes 7680
  28.3 18.8 %collective-permute-done.7 = bf16[2,256,960]{1,2,0:T(8,128)(2,1)} collective-permute-done((bf16[2,256,960]{1,2,0:T(8,128)(2,1)S(1)}, bf16[2,256,960]{1,2,0:T(8,128)(2,1)}, u32[]{:S(2)}, u32[]{:S(2)}) %collective-permute-start.7) | collective-permute-done | bytes 983072 | tf_op jit(solution)/shard_map/ppermute | solution.py:282
  53.0 5.9 %collective-permute-start.3 = (bf16[640,512]{1,0:T(8,128)(2,1)S(1)}, bf16[640,512]{1,0:T(8,128)(2,1)S(1)}, u32[]{:S(2)}, u32[]{:S(2)}) collective-permute-start(bf16[640,512]{1,0:T(8,128)(2,1)S(1)} %pad_maximum_fusion.8), channel_id=1, source_target_pairs={{0,6},{1,7},{8,14},{9,15},{16,22},{17,23},{24,30},{25,31}} | collective-permute-start | bytes 1966088 | tf_op jit(solution)/shard_map/ppermute | solution.py:229
  64.6 9.5 %collective-permute-done.3 = bf16[640,512]{1,0:T(8,128)(2,1)S(1)} collective-permute-done((bf16[640,512]{1,0:T(8,128)(2,1)S(1)}, bf16[640,512]{1,0:T(8,128)(2,1)S(1)}, u32[]{:S(2)}, u32[]{:S(2)}) %collective-permute-start.3) | collective-permute-done | bytes 655392 | tf_op jit(solution)/shard_map/ppermute | solution.py:229
  74.1 14.0 %collective-permute-done.2 = bf16[640,512]{1,0:T(8,128)(2,1)S(1)} collective-permute-done((bf16[640,512]{1,0:T(8,128)(2,1)S(1)}, bf16[640,512]{1,0:T(8,128)(2,1)S(1)}, u32[]{:S(2)}, u32[]{:S(2)}) %collective-permute-start.2) | collective-permute-done | bytes 655392 | tf_op jit(solution)/shard_map/ppermute | solution.py:229
  88.1 12.0 %collective-permute-done.1 = bf16[640,512]{1,0:T(8,128)(2,1)S(1)} collective-permute-done((bf16[640,512]{1,0:T(8,128)(2,1)S(1)}, bf16[640,512]{1,0:T(8,128)(2,1)S(1)}, u32[]{:S(2)}, u32[]{:S(2)}) %collective-permute-start.1) | collective-permute-done | bytes 655392 | tf_op jit(solution)/shard_map/ppermute | solution.py:229
  100.5 7.4 %attend_forward.1 = (bf16[15,64,512]{2,1,0:T(8,128)(2,1)S(1)}, f32[15,1,512]{2,1,0:T(1,128)S(1)}) custom-call(bf16[15,64,512]{2,1,0:T(8,128)(2,1)S(1)} %bitcast.222, bf16[4,2,5,64,512]{4,3,2,1,0:T(8,128)(2,1)S(1)} %pad_maximum_fusion.key_ref.value_ref, bf16[4,2,5,64,512]{4,3,2,1,0:T(8,128)(2,1)S(1)} %pad_maximum_fusion.key_ref.value_ref), custom_call_target="tpu_custom_call" | custom-call | flops 16106127360 | bytes 2949120 | tf_op jit(solution)/shard_map/attend_forward/pallas_call | solution.py:110
  126.2 17.3 %all-gather.14.cloned.1.call-done = bf16[960,1280]{1,0:T(8,128)(2,1)} async-done(((bf16[240,1280]{1,0:T(8,128)(2,1)}), bf16[960,1280]{1,0:T(8,128)(2,1)}) %all-gather.14.cloned.1.call-update) | async-done | bytes 2457616 | tf_op jit(solution)/shard_map/all_gather | solution.py:301
  143.6 5.9 %multiply_convert_fusion.2 = (bf16[512,1280]{1,0:T(8,128)(2,1)S(1)}, bf16[512,1280]{1,0:T(8,128)(2,1)S(1)}, bf16[512,1280]{1,0:T(8,128)(2,1)S(1)}) fusion(f32[512,1280]{1,0:T(8,128)} %fusion.55, f32[512,1280]{1,0:T(8,128)} %fusion.56, bf16[960,1280]{1,0:T(8,128)(2,1)} %all-gather.14.cloned.1.call-done, bf16[256,960]{0,1:T(8,128)(2,1)} %get-tuple-element.39, ...), kind=kOutput, calls=%fused_computation.14 | convolution fusion | flops 1270087680 | bytes 12615680 | tf_op jit(solution)/shard_map/dot_general | solution.py:23
  188.3 8.0 %collective-permute-done.8 = bf16[512,960]{0,1:T(8,128)(2,1)S(1)} collective-permute-done((bf16[512,960]{0,1:T(8,128)(2,1)S(1)}, bf16[512,960]{0,1:T(8,128)(2,1)S(1)}, u32[]{:S(2)}, u32[]{:S(2)}) %collective-permute-start.8) | collective-permute-done | bytes 983072 | tf_op jit(solution)/shard_map/ppermute | solution.py:282
  202.0 8.4 %attend_backward.2 = (bf16[9,64,512]{2,1,0:T(8,128)(2,1)S(1)}, bf16[4,2,3,64,512]{4,3,2,1,0:T(8,128)(2,1)S(1)}) custom-call(bf16[15,64,512]{2,1,0:T(8,128)(2,1)S(1)} %bitcast.223, bf16[4,2,5,64,512]{4,3,2,1,0:T(8,128)(2,1)S(1)} %pad_maximum_fusion.key_ref.value_ref, bf16[4,2,5,64,512]{4,3,2,1,0:T(8,128)(2,1)S(1)} %pad_maximum_fusion.key_ref.value_ref, ...), custom_call_target="tpu_custom_call" | custom-call | flops 24159191040 | bytes 4915200 | tf_op jit(solution)/shard_map/attend_backward/pallas_call | solution.py:195
  244.9 49.7 %collective-permute-done.14 = bf16[256,512]{1,0:T(8,128)(2,1)S(1)} collective-permute-done((bf16[256,512]{1,0:T(8,128)(2,1)}, bf16[256,512]{1,0:T(8,128)(2,1)S(1)}, u32[]{:S(2)}, u32[]{:S(2)}) %collective-permute-start.14) | collective-permute-done | bytes 262176 | tf_op jit(solution)/shard_map/ppermute | solution.py:229
  295.9 13.7 %collective-permute-done.13 = bf16[256,512]{1,0:T(8,128)(2,1)S(1)} collective-permute-done((bf16[256,512]{1,0:T(8,128)(2,1)S(1)}, bf16[256,512]{1,0:T(8,128)(2,1)S(1)}, u32[]{:S(2)}, u32[]{:S(2)}) %collective-permute-start.13) | collective-permute-done | bytes 262176 | tf_op jit(solution)/shard_map/ppermute | solution.py:229
  333.0 6.0 %concatenate.61 = bf16[960,1602]{1,0:T(8,128)(2,1)} concatenate(bf16[960,1600]{1,0:T(8,128)(2,1)} %convolution_convert_fusion, bf16[960,1]{1,0:T(8,128)(2,1)S(1)} %broadcast_in_dim.14, bf16[960,1]{1,0:T(8,128)(2,1)S(1)} %broadcast_in_dim.15), dimensions={1} | concatenate | bytes 6151680 | tf_op jit(solution)/shard_map/concatenate | solution.py:409
  342.0 7.9 %collective-permute-start.24 = (bf16[120,1280]{1,0:T(8,128)(2,1)S(1)}, bf16[120,1280]{1,0:T(8,128)(2,1)S(1)}, u32[]{:S(2)}, u32[]{:S(2)}) collective-permute-start(bf16[120,1280]{1,0:T(8,128)(2,1)S(1)} %select_bitcast_fusion.14), channel_id=1, source_target_pairs={{0,2},{2,0},{4,6},{6,4},{1,3},{3,1},{5,7},{7,5},{8,10},{10,8},{12,... | collective-permute-start | bytes 921608 | tf_op jit(solution)/shard_map/ppermute | solution.py:234
  370.4 16.1 %collective-permute-done.17 = bf16[1,240,960]{2,1,0:T(8,128)(2,1)S(1)} collective-permute-done((bf16[1,240,960]{2,1,0:T(8,128)(2,1)S(1)}, bf16[1,240,960]{2,1,0:T(8,128)(2,1)S(1)}, u32[]{:S(2)}, u32[]{:S(2)}) %collective-permute-start.17) | collective-permute-done | bytes 460832 | tf_op jit(solution)/shard_map/ppermute | solution.py:234
  386.8 7.3 %collective-permute-done.25 = bf16[120,1280]{1,0:T(8,128)(2,1)S(1)} collective-permute-done((bf16[120,1280]{1,0:T(8,128)(2,1)S(1)}, bf16[120,1280]{1,0:T(8,128)(2,1)S(1)}, u32[]{:S(2)}, u32[]{:S(2)}) %collective-permute-start.25) | collective-permute-done | bytes 307232 | tf_op jit(solution)/shard_map/ppermute | solution.py:234
  394.3 6.4 %collective-permute-done.30 = bf16[120,1280]{1,0:T(8,128)(2,1)S(1)} collective-permute-done((bf16[120,1280]{1,0:T(8,128)(2,1)S(1)}, bf16[120,1280]{1,0:T(8,128)(2,1)S(1)}, u32[]{:S(2)}, u32[]{:S(2)}) %collective-permute-start.30) | collective-permute-done | bytes 307232 | tf_op jit(solution)/shard_map/ppermute | solution.py:234
  412.2 5.9 %collective-permute-done.26 = bf16[120,1280]{1,0:T(8,128)(2,1)S(1)} collective-permute-done((bf16[120,1280]{1,0:T(8,128)(2,1)S(1)}, bf16[120,1280]{1,0:T(8,128)(2,1)S(1)}, u32[]{:S(2)}, u32[]{:S(2)}) %collective-permute-start.26) | collective-permute-done | bytes 307232 | tf_op jit(solution)/shard_map/ppermute | solution.py:234
  418.2 6.5 %collective-permute-done.31 = bf16[120,1280]{1,0:T(8,128)(2,1)S(1)} collective-permute-done((bf16[120,1280]{1,0:T(8,128)(2,1)S(1)}, bf16[120,1280]{1,0:T(8,128)(2,1)S(1)}, u32[]{:S(2)}, u32[]{:S(2)}) %collective-permute-start.31) | collective-permute-done | bytes 307232 | tf_op jit(solution)/shard_map/ppermute | solution.py:234
  424.7 6.1 %collective-permute-done.36 = bf16[120,1280]{1,0:T(8,128)(2,1)S(1)} collective-permute-done((bf16[120,1280]{1,0:T(8,128)(2,1)S(1)}, bf16[120,1280]{1,0:T(8,128)(2,1)S(1)}, u32[]{:S(2)}, u32[]{:S(2)}) %collective-permute-start.36) | collective-permute-done | bytes 307232 | tf_op jit(solution)/shard_map/ppermute | solution.py:234
  433.3 20.1 %collective-permute-done.20 = bf16[120,960]{1,0:T(8,128)(2,1)S(1)} collective-permute-done((bf16[120,960]{1,0:T(8,128)(2,1)S(1)}, bf16[120,960]{1,0:T(8,128)(2,1)S(1)}, u32[]{:S(2)}, u32[]{:S(2)}) %collective-permute-start.20) | collective-permute-done | bytes 230432 | tf_op jit(solution)/shard_map/ppermute | solution.py:234
  454.6 6.6 %collective-permute-done.21 = bf16[120,960]{1,0:T(8,128)(2,1)S(1)} collective-permute-done((bf16[120,960]{1,0:T(8,128)(2,1)S(1)}, bf16[120,960]{1,0:T(8,128)(2,1)S(1)}, u32[]{:S(2)}, u32[]{:S(2)}) %collective-permute-start.21) | collective-permute-done | bytes 230432 | tf_op jit(solution)/shard_map/ppermute | solution.py:234
  462.3 48.5 %all-reduce.5.cloned.1.call-done = bf16[240,1602]{1,0:T(8,128)(2,1)} async-done(((bf16[240,1602]{1,0:T(8,128)(2,1)}), bf16[240,1602]{1,0:T(8,128)(2,1)}) %all-reduce.5.cloned.1.call-update) | async-done | bytes 768976 | tf_op jit(solution)/shard_map/psum | solution.py:410
  (311 shorter events, 190.7 us)
Async XLA Ops:
  7.2 42.4 %all-gather.6.cloned.1.call-start = ((), (), s32[]{:S(2)}) async-start(), calls=%async_computation.1 | async-start | bytes 3993600 | tf_op jit(solution)/shard_map/all_gather | solution.py:297
  9.5 99.3 %all-gather.8.cloned.1.call-start = ((), (), s32[]{:S(2)}) async-start(), calls=%async_computation.2 | async-start | bytes 2457600 | tf_op jit(solution)/shard_map/all_gather | solution.py:298
  10.3 105.7 %all-gather.10.cloned.1.call-start = ((), (), s32[]{:S(2)}) async-start(), calls=%async_computation.3 | async-start | bytes 3072000 | tf_op jit(solution)/shard_map/all_gather | solution.py:299
  11.0 110.1 %all-gather.12.cloned.1.call-start = ((), (), s32[]{:S(2)}) async-start(), calls=%async_computation.4 | async-start | bytes 3072000 | tf_op jit(solution)/shard_map/all_gather | solution.py:300
  11.6 132.0 %all-gather.14.cloned.1.call-start = ((), (), s32[]{:S(2)}) async-start(), calls=%async_computation.5 | async-start | bytes 3072000 | tf_op jit(solution)/shard_map/all_gather | solution.py:301
  14.7 32.4 %collective-permute-start.7 = (bf16[2,256,960]{1,2,0:T(8,128)(2,1)S(1)}, bf16[2,256,960]{1,2,0:T(8,128)(2,1)}, u32[]{:S(2)}, u32[]{:S(2)}) collective-permute-start(bf16[2,256,960]{1,2,0:T(8,128)(2,1)S(1)} %copy-done.38), channel_id=1, source_target_pairs={{0,1},{1,0},{2,3},{3,2},{4,5},{5,4},{6,7},{7,6},{8,9},{9,8},{10,11... | collective-permute-start | bytes 2949128 | tf_op jit(solution)/shard_map/ppermute | solution.py:282
  14.8 418.4 %reduce-scatter.2.cloned.1.call-start = ((), (), s32[]{:S(2)}) async-start(), calls=%async_computation.6 | async-start | bytes 3993600 | tf_op jit(solution)/shard_map/reduce_scatter | solution.py:411
  60.2 39.9 %collective-permute-start.1 = (bf16[640,512]{1,0:T(8,128)(2,1)S(1)}, bf16[640,512]{1,0:T(8,128)(2,1)S(1)}, u32[]{:S(2)}, u32[]{:S(2)}) collective-permute-start(bf16[640,512]{1,0:T(8,128)(2,1)S(1)} %pad_maximum_fusion.8), channel_id=1, source_target_pairs={{0,2},{2,4},{4,6},{1,3},{3,5},{5,7},{8,10},{10,12},{12,14},{9,11},... | collective-permute-start | bytes 1966088 | tf_op jit(solution)/shard_map/ppermute | solution.py:229
  114.5 43.9 %collective-permute-start.4 = (bf16[512,960]{0,1:T(8,128)(2,1)}, bf16[512,960]{0,1:T(8,128)(2,1)}, u32[]{:S(2)}, u32[]{:S(2)}) collective-permute-start(bf16[512,960]{0,1:T(8,128)(2,1)} %multiply_convert_fusion.6), channel_id=1, source_target_pairs={{0,1},{1,0},{2,3},{3,2},{4,5},{5,4},{6,7},{7,6},{8,9},{9,8},{10,11... | collective-permute-start | bytes 2949128 | tf_op jit(solution)/shard_map/ppermute | solution.py:282
  175.7 46.0 %collective-permute-start.5 = (bf16[512,960]{0,1:T(8,128)(2,1)}, bf16[512,960]{0,1:T(8,128)(2,1)}, u32[]{:S(2)}, u32[]{:S(2)}) collective-permute-start(bf16[512,960]{0,1:T(8,128)(2,1)} %convolution_convert_fusion.3), channel_id=1, source_target_pairs={{0,1},{1,0},{2,3},{3,2},{4,5},{5,4},{6,7},{7,6},{8,9},{9,8},{10,11... | collective-permute-start | bytes 2949128 | tf_op jit(solution)/shard_map/ppermute | solution.py:282
  180.7 51.1 %collective-permute-start.22 = (bf16[2,240,1280]{2,1,0:T(8,128)(2,1)}, bf16[2,240,1280]{2,1,0:T(8,128)(2,1)}, u32[]{:S(2)}, u32[]{:S(2)}) collective-permute-start(bf16[2,240,1280]{2,1,0:T(8,128)(2,1)} %select_bitcast_fusion.2), channel_id=1, source_target_pairs={{0,8},{8,0},{16,24},{24,16},{1,9},{9,1},{17,25},{25,17},{2,10},{10... | collective-permute-start | bytes 3686408 | tf_op jit(solution)/shard_map/ppermute | solution.py:234
  185.2 50.9 %collective-permute-start.27 = (bf16[2,240,1280]{2,1,0:T(8,128)(2,1)}, bf16[2,240,1280]{2,1,0:T(8,128)(2,1)}, u32[]{:S(2)}, u32[]{:S(2)}) collective-permute-start(bf16[2,240,1280]{2,1,0:T(8,128)(2,1)} %select_bitcast_fusion.1), channel_id=1, source_target_pairs={{0,8},{8,0},{16,24},{24,16},{1,9},{9,1},{17,25},{25,17},{2,10},{10... | collective-permute-start | bytes 3686408 | tf_op jit(solution)/shard_map/ppermute | solution.py:234
  188.3 52.5 %collective-permute-start.32 = (bf16[2,240,1280]{2,1,0:T(8,128)(2,1)}, bf16[2,240,1280]{2,1,0:T(8,128)(2,1)}, u32[]{:S(2)}, u32[]{:S(2)}) collective-permute-start(bf16[2,240,1280]{2,1,0:T(8,128)(2,1)} %select_bitcast_fusion), channel_id=1, source_target_pairs={{0,8},{8,0},{16,24},{24,16},{1,9},{9,1},{17,25},{25,17},{2,10},{10... | collective-permute-start | bytes 3686408 | tf_op jit(solution)/shard_map/ppermute | solution.py:234
  219.1 92.3 %collective-permute-start.11 = (bf16[384,512]{1,0:T(8,128)(2,1)}, bf16[384,512]{1,0:T(8,128)(2,1)}, u32[]{:S(2)}, u32[]{:S(2)}) collective-permute-start(bf16[384,512]{1,0:T(8,128)(2,1)} %bitcast.28), channel_id=1, source_target_pairs={{6,0},{7,1},{14,8},{15,9},{22,16},{23,17},{30,24},{31,25}} | collective-permute-start | bytes 1179656 | tf_op jit(solution)/shard_map/ppermute | solution.py:229
  221.6 90.3 %collective-permute-start.10 = (bf16[384,512]{1,0:T(8,128)(2,1)}, bf16[384,512]{1,0:T(8,128)(2,1)}, u32[]{:S(2)}, u32[]{:S(2)}) collective-permute-start(bf16[384,512]{1,0:T(8,128)(2,1)} %bitcast.27), channel_id=1, source_target_pairs={{4,0},{6,2},{5,1},{7,3},{12,8},{14,10},{13,9},{15,11},{20,16},{22,... | collective-permute-start | bytes 1179656 | tf_op jit(solution)/shard_map/ppermute | solution.py:229
  231.8 62.8 %collective-permute-start.14 = (bf16[256,512]{1,0:T(8,128)(2,1)}, bf16[256,512]{1,0:T(8,128)(2,1)S(1)}, u32[]{:S(2)}, u32[]{:S(2)}) collective-permute-start(bf16[256,512]{1,0:T(8,128)(2,1)} %bitcast.255), channel_id=1, source_target_pairs={{6,0},{7,1},{14,8},{15,9},{22,16},{23,17},{30,24},{31,25}} | collective-permute-start | bytes 786440 | tf_op jit(solution)/shard_map/ppermute | solution.py:229
  236.4 73.2 %collective-permute-start.13 = (bf16[256,512]{1,0:T(8,128)(2,1)S(1)}, bf16[256,512]{1,0:T(8,128)(2,1)S(1)}, u32[]{:S(2)}, u32[]{:S(2)}) collective-permute-start(bf16[256,512]{1,0:T(8,128)(2,1)S(1)} %bitcast.254), channel_id=1, source_target_pairs={{4,0},{6,2},{5,1},{7,3},{12,8},{14,10},{13,9},{15,11},{20,16},{22,... | collective-permute-start | bytes 786440 | tf_op jit(solution)/shard_map/ppermute | solution.py:229
  240.8 68.8 %collective-permute-start.12 = (bf16[256,512]{1,0:T(8,128)(2,1)S(1)}, bf16[256,512]{1,0:T(8,128)(2,1)S(1)}, u32[]{:S(2)}, u32[]{:S(2)}) collective-permute-start(bf16[256,512]{1,0:T(8,128)(2,1)S(1)} %bitcast.253), channel_id=1, source_target_pairs={{2,0},{4,2},{6,4},{3,1},{5,3},{7,5},{10,8},{12,10},{14,12},{11,9},... | collective-permute-start | bytes 786440 | tf_op jit(solution)/shard_map/ppermute | solution.py:229
  309.6 50.2 %collective-permute-start.16 = (bf16[2,240,960]{2,1,0:T(8,128)(2,1)}, bf16[2,240,960]{2,1,0:T(8,128)(2,1)}, u32[]{:S(2)}, u32[]{:S(2)}) collective-permute-start(bf16[2,240,960]{2,1,0:T(8,128)(2,1)} %select_bitcast_fusion.3), channel_id=1, source_target_pairs={{0,8},{8,0},{16,24},{24,16},{1,9},{9,1},{17,25},{25,17},{2,10},{10... | collective-permute-start | bytes 2764808 | tf_op jit(solution)/shard_map/ppermute | solution.py:234
  311.4 30.7 %collective-permute-start.28 = (bf16[1,240,1280]{2,1,0:T(8,128)(2,1)}, bf16[1,240,1280]{2,1,0:T(8,128)(2,1)}, u32[]{:S(2)}, u32[]{:S(2)}) collective-permute-start(bf16[1,240,1280]{2,1,0:T(8,128)(2,1)} %select_bitcast_fusion.5), channel_id=1, source_target_pairs={{0,16},{8,24},{16,0},{24,8},{1,17},{9,25},{17,1},{25,9},{2,18},{10... | collective-permute-start | bytes 1843208 | tf_op jit(solution)/shard_map/ppermute | solution.py:234
  312.0 40.5 %collective-permute-start.33 = (bf16[1,240,1280]{2,1,0:T(8,128)(2,1)}, bf16[1,240,1280]{2,1,0:T(8,128)(2,1)}, u32[]{:S(2)}, u32[]{:S(2)}) collective-permute-start(bf16[1,240,1280]{2,1,0:T(8,128)(2,1)} %select_bitcast_fusion.4), channel_id=1, source_target_pairs={{0,16},{8,24},{16,0},{24,8},{1,17},{9,25},{17,1},{25,9},{2,18},{10... | collective-permute-start | bytes 1843208 | tf_op jit(solution)/shard_map/ppermute | solution.py:234
  339.0 171.7 %all-reduce.5.cloned.1.call-start = ((), (), s32[]{:S(2)}) async-start(), calls=%async_computation.7 | async-start | bytes 1597440 | tf_op jit(solution)/shard_map/psum | solution.py:410
  364.4 36.3 %collective-permute-start.30 = (bf16[120,1280]{1,0:T(8,128)(2,1)S(1)}, bf16[120,1280]{1,0:T(8,128)(2,1)S(1)}, u32[]{:S(2)}, u32[]{:S(2)}) collective-permute-start(bf16[120,1280]{1,0:T(8,128)(2,1)S(1)} %fusion.34), channel_id=1, source_target_pairs={{0,4},{2,6},{4,0},{6,2},{1,5},{3,7},{5,1},{7,3},{8,12},{10,14},{12... | collective-permute-start | bytes 921608 | tf_op jit(solution)/shard_map/ppermute | solution.py:234
  369.2 37.0 %collective-permute-start.35 = (bf16[120,1280]{1,0:T(8,128)(2,1)S(1)}, bf16[120,1280]{1,0:T(8,128)(2,1)S(1)}, u32[]{:S(2)}, u32[]{:S(2)}) collective-permute-start(bf16[120,1280]{1,0:T(8,128)(2,1)S(1)} %fusion.33), channel_id=1, source_target_pairs={{0,4},{2,6},{4,0},{6,2},{1,5},{3,7},{5,1},{7,3},{8,12},{10,14},{12... | collective-permute-start | bytes 921608 | tf_op jit(solution)/shard_map/ppermute | solution.py:234
  (75 other events, 1050.4 us)
Sparse Core Ops, SparseCore 0:
  10.2 31.5 all-gather.5
  43.3 21.8 all-gather.7
  66.8 24.6 all-gather.9
  92.8 24.6 all-gather.11
  118.9 24.6 all-gather.13
  339.2 54.0 reduce-scatter.1
  433.4 77.3 all-reduce.4
